TPU v7x, 256 devices: a whole 4x4x8 slice. The times are simulated.
256 devices in a mesh: grp: 2 (over x_lo), dp: 32 (over y, z), mp: 4 (over x_hi, core).
Axes of the slice: x: 4 (x_hi: 2, x_lo: 2; x = x_hi * 2 + x_lo), y: 4, z: 8, core: 2. Of those that a mesh axis runs over, the one named last changes fastest.
Arguments:
- pooled: bfloat16 [32, 8, 4096, 128], P('dp', ('grp', 'mp')), may hold values from -32 to 32
- counts: int32 [32, 8, 4096], P('dp', ('grp', 'mp')), may hold values from 0 to 7
- sample_order: int32 [8, 4096], P(('grp', 'mp')), may hold values from 0 to 4095, each once within a row
- table_order: int32 [32], replicated, may hold values from 0 to 31, each once
- teacher_w1: bfloat16 [4096, 2048], P(None, ('grp', 'mp')), may hold values from -0.09375 to 0.09375
- teacher_w2: bfloat16 [2048, 2048], P(('grp', 'mp')), may hold values from -0.125 to 0.125
- projection: bfloat16 [2048, 512], replicated, may hold values from -0.125 to 0.125
- student_w1: bfloat16 [4096, 512], replicated, may hold values from -0.09375 to 0.09375
- student_w2: bfloat16 [512, 512], replicated, may hold values from -0.25 to 0.25
Outputs:
- grad_w1: float32 [4096, 512], P(('grp', 'dp', 'mp'))
- grad_w2: float32 [512, 512], replicated
- sample_loss: float32 [8, 4096], P(('grp', 'mp'), 'dp')
Inputs may be any that keep to these rules, and one draw needn't show every extreme that they name: `sample_order`: each row is a permutation; slot i of block q lies on dp index i // 128. `table_order`: a permutation; storage slot s lies on dp index s.
All inputs are finite; a program needn't handle non-finite values.
Results may differ from a plain program's by a relative error of at most 0.0085.
The roundings to bfloat16 on the way count: a program that leaves them out, or rounds other values in their place, can miss the bound.
Values may be sent and summed in bfloat16 or wider, within the bound.
No kernel may reach another device: no remote copies, remote signals or barrier semaphores. Data moves between devices by JAX's collectives and lax.ppermute only.
A program may use at most 128 MiB of HBM per device.

v0:
```python
import jax
import jax.numpy as jnp
from jax import lax
from jax.sharding import PartitionSpec as P


def contract_rows(left, right):
    return lax.dot_general(
        left, right, (((0,), (0,)), ((), ())), preferred_element_type=jnp.float32
    )


def split_parts(values, pieces):
    parts = []
    remain = values
    for index in range(pieces):
        upper = lax.optimization_barrier(remain.astype(jnp.bfloat16))
        parts.append(upper)
        remain = remain - upper.astype(jnp.float32)
    return parts


def exact_product(values, weights):
    total = None
    for part in split_parts(values, 3):
        term = jnp.dot(part, weights, preferred_element_type=jnp.float32)
        total = term if total is None else total + term
    return total


def shards(
    pooled,
    counts,
    sample_order,
    table_order,
    teacher_w1,
    teacher_w2,
    projection,
    student_w1,
    student_w2,
):
    divisor = jnp.maximum(counts[:, 0], 1).astype(jnp.float32)
    averaged = (pooled[:, 0].astype(jnp.float32) / divisor[..., None]).astype(jnp.bfloat16)
    ordered = jnp.take(averaged, sample_order[0], axis=1)
    outgoing = jnp.transpose(ordered, (1, 0, 2))
    arrived = lax.all_to_all(outgoing, "dp", split_axis=0, concat_axis=1, tiled=True)
    samples = arrived.shape[0]
    tables = arrived.shape[1]
    inverse = (
        jnp.zeros((tables,), jnp.int32).at[table_order].set(jnp.arange(tables, dtype=jnp.int32))
    )
    features = jnp.take(arrived, inverse, axis=1).reshape(samples, tables * arrived.shape[2])
    teacher_hidden = jax.nn.relu(
        jnp.dot(
            lax.all_gather(features, ("grp", "mp"), axis=0, tiled=True),
            teacher_w1,
            preferred_element_type=jnp.float32,
        )
    ).astype(jnp.bfloat16)
    teacher_rows = lax.psum_scatter(
        jnp.dot(teacher_hidden, teacher_w2, preferred_element_type=jnp.float32),
        ("grp", "mp"),
        scatter_dimension=0,
        tiled=True,
    )
    target = exact_product(teacher_rows, projection)
    student_pre = jnp.dot(features, student_w1, preferred_element_type=jnp.float32)
    student_hidden = jax.nn.relu(student_pre).astype(jnp.bfloat16)
    student_out = jnp.dot(student_hidden, student_w2, preferred_element_type=jnp.float32)
    difference = student_out - target
    sample_loss = (0.5 * jnp.mean(difference * difference, axis=1)).reshape(1, samples)
    devices = lax.axis_size("grp") * lax.axis_size("dp") * lax.axis_size("mp")
    grad_scale = 8192.0 / (samples * devices * student_w2.shape[1])
    out_grad = (grad_scale * difference).astype(jnp.bfloat16)
    grad_w2 = lax.psum(contract_rows(student_hidden, out_grad), ("grp", "dp", "mp"))
    back = jnp.dot(out_grad, student_w2.T, preferred_element_type=jnp.float32)
    hidden_grad = jnp.where(student_pre > 0, back, 0.0).astype(jnp.bfloat16)
    grad_w1 = lax.psum_scatter(
        contract_rows(features, hidden_grad), ("grp", "dp", "mp"), scatter_dimension=0, tiled=True
    )
    return (grad_w1, grad_w2, sample_loss)


def solution(mesh):
    return jax.shard_map(
        shards,
        mesh=mesh,
        in_specs=(
            P("dp", ("grp", "mp"), None, None),
            P("dp", ("grp", "mp"), None),
            P(("grp", "mp"), None),
            P(),
            P(None, ("grp", "mp")),
            P(("grp", "mp"), None),
            P(),
            P(),
            P(),
        ),
        out_specs=(P(("grp", "dp", "mp"), None), P(), P(("grp", "mp"), "dp")),
        check_vma=False,
    )
```

profile of v0, /device:TPU:32, one launch (start us, length us, event | category | flops | bytes accessed | tf_op | source)
XLA Modules:
  0.0 1837.3 jit_solution(25737887137886696)
XLA Ops:
  9.5 1.8 fusion.6
  11.3 15.0 gather_fusion
  26.4 3.4 bitcast_select_fusion.1
  30.2 2.1 reduce
  32.3 2.1 reshape.175
  34.5 11.4 all-to-all-start
  46.7 27.7 %all-to-all-done = bf16[32,2,8192]{2,1,0:T(2,128)(2,1)S(1)} async-done(((bf16[32,2,8192]{2,1,0:T(2,128)(2,1)}), bf16[32,2,8192]{2,1,0:T(2,128)(2,1)S(1)}, u32[]{:S(2)}, u32[]{:S(2)}) %all-to-all-start) | async-done | bytes 1048608 | tf_op jit(solution)/shard_map/all_to_all | solution.py:46
  74.4 3.4 reshape.176
  77.8 1.7 copy.17
  79.5 1.7 gather_fusion.1
  81.2 1.6 copy.16
  82.8 2.9 bitcast_select_fusion
  85.8 97.1 %all-gather.2.cloned.1.call-done = bf16[1024,4096]{0,1:T(8,128)(2,1)} async-done(((bf16[128,4096]{0,1:T(8,128)(2,1)}), bf16[1024,4096]{0,1:T(8,128)(2,1)}) %all-gather.2.cloned.1.call-update) | async-done | bytes 8388624 | tf_op jit(solution)/shard_map/all_gather | solution.py:55
  182.8 12.3 fusion.2
  195.2 1.1 copy-done.2
  196.3 3.0 fusion.22
  200.3 90.9 %reduce-scatter.3.cloned.1.call-done = f32[128,2048]{1,0:T(8,128)} async-done(((f32[1024,2048]{1,0:T(8,128)}), f32[128,2048]{1,0:T(8,128)}) %reduce-scatter.3.cloned.1.call-update) | async-done | bytes 1048592 | tf_op jit(solution)/shard_map/reduce_scatter | solution.py:60
  291.2 1.4 convert_element_type.71
  292.6 2.2 fusion.23
  297.6 1.3 fusion.11
  298.9 5.9 fusion.5
  305.4 246.6 %all-reduce.2.cloned.1.call-done = f32[512,512]{1,0:T(8,128)} async-done(((f32[512,512]{1,0:T(8,128)}), f32[512,512]{1,0:T(8,128)}) %all-reduce.2.cloned.1.call-update) | async-done | bytes 1048592 | tf_op jit(solution)/shard_map/psum | solution.py:75
  552.0 1276.5 %reduce-scatter.5.cloned.1.call-done = f32[16,512]{1,0:T(8,128)} async-done(((f32[4096,512]{1,0:T(8,128)}), f32[16,512]{1,0:T(8,128)}) %reduce-scatter.5.cloned.1.call-update) | async-done | bytes 32784 | tf_op jit(solution)/shard_map/reduce_scatter | solution.py:78
  1828.5 2.3 copy.20
  (41 shorter events, 8.1 us)
Async XLA Ops:
  7.2 175.7 %copy-start = (bf16[4096,256]{1,0:T(8,128)(2,1)S(1)}, bf16[4096,256]{1,0:T(8,128)(2,1)}, u32[]{:S(2)}) copy-start(bf16[4096,256]{1,0:T(8,128)(2,1)} %param.13) | copy-start | bytes 6291460
  32.3 13.6 copy-start.7
  34.5 39.9 %all-to-all-start = ((bf16[32,2,8192]{2,1,0:T(2,128)(2,1)}), bf16[32,2,8192]{2,1,0:T(2,128)(2,1)S(1)}, u32[]{:S(2)}, u32[]{:S(2)}) async-start(bf16[32,2,8192]{2,1,0:T(2,128)(2,1)} %reshape.175), calls=%async_computation | async-start | bytes 2097152 | tf_op jit(solution)/shard_map/all_to_all | solution.py:46
  45.8 137.0 %all-gather.2.cloned.1.call-start = ((), (), s32[]{:S(2)}) async-start(), calls=%async_computation.3 | async-start | bytes 9437184 | tf_op jit(solution)/shard_map/all_gather | solution.py:55
  85.7 205.5 %reduce-scatter.3.cloned.1.call-start = ((), (), s32[]{:S(2)}) async-start(), calls=%async_computation.4 | async-start | bytes 9437184 | tf_op jit(solution)/shard_map/reduce_scatter | solution.py:60
  195.1 1.2 copy-start.2
  195.1 356.9 %all-reduce.2.cloned.1.call-start = ((), (), s32[]{:S(2)}) async-start(), calls=%async_computation.6 | async-start | bytes 2097152 | tf_op jit(solution)/shard_map/psum | solution.py:75
  196.3 3.0 copy-start.5
  291.2 3.6 copy-start.3
  292.6 2.3 copy-start.1
  295.4 1.0 copy-start.6
  296.9 0.7 copy-start.4
  298.9 1529.6 %reduce-scatter.5.cloned.1.call-start = ((), (), s32[]{:S(2)}) async-start(), calls=%async_computation.5 | async-start | bytes 8421376 | tf_op jit(solution)/shard_map/reduce_scatter | solution.py:78
Sparse Core Ops, SparseCore 0:
  85.8 96.9 all-gather.1
  195.3 95.8 reduce-scatter.2
  299.0 252.9 all-reduce.1
  555.1 1273.3 reduce-scatter.4
where the time goes:
time: 1850 us; the launch traced here: 1840 us
  waiting for transfers between devices  1740 us (94%)
  local copies, waits for them, and re-layouts  31.7 us (2%)
  matrix products  26.6 us (1%)
    reduce_scatter x1, waiting for transfers between devices, shards(): lax.psum_scatter(contract_rows(features, hidden_grad), ('grp', 'dp', 'mp'...  1280 us
    psum x1, waiting for transfers between devices, shards(): lax.psum(contract_rows(student_hidden, out_grad), ('grp', 'dp', 'mp'))  247 us
    all_gather x1, waiting for transfers between devices, shards(): lax.all_gather(features, ('grp', 'mp'), axis=0, tiled=True)  97.1 us
    reduce_scatter x1, waiting for transfers between devices, shards(): lax.psum_scatter(jnp.dot(teacher_hidden, teacher_w2, preferred_element_ty...  90.9 us
  transfers between devices with their start and end apart: 5, of which 5 were waited for; matrix products, arithmetic and copies ran while one was open for 1% of the time, Pallas kernels for 0%

commit v1 on v0

v1 whole, which is shorter than its diff:
```python
import jax
import jax.numpy as jnp
from jax import lax
from jax.experimental import pallas as pl
from jax.experimental.pallas import tpu as pltpu
from jax.sharding import PartitionSpec as P

LINE = ("grp", "mp")
CORE, NEAR, FAR, OPPOSITE = 1, 4, 6, 2

smem = pl.BlockSpec(memory_space=pltpu.SMEM)
vmem = pl.BlockSpec(memory_space=pltpu.VMEM)
LIMIT = pltpu.CompilerParams(vmem_limit_bytes=40 * 1024 * 1024)


def dot(left, right):
    return jnp.dot(left, right, preferred_element_type=jnp.float32)


def swap(values, mask):
    return lax.ppermute(values, LINE, [(index, index ^ mask) for index in range(8)])


def split_two(values):
    upper = lax.optimization_barrier(values.astype(jnp.bfloat16))
    lower = (values - upper.astype(jnp.float32)).astype(jnp.bfloat16)
    return jnp.concatenate([upper, lower], axis=0)


def order_kernel(order_ref, averaged_ref, ordered_ref):
    step = 64

    @pl.loop(0, ordered_ref.shape[0] // step)
    def _(index):
        base = pl.multiple_of(index * step, step)
        rows = [averaged_ref[pl.ds(order_ref[0, base + row], 1), :] for row in range(step)]
        ordered_ref[pl.ds(base, step), :] = jnp.concatenate(rows, axis=0).astype(jnp.bfloat16)


def take_rows(averaged, order):
    return pl.pallas_call(
        order_kernel,
        out_shape=jax.ShapeDtypeStruct(averaged.shape, jnp.bfloat16),
        in_specs=[smem, vmem],
        out_specs=vmem,
        compiler_params=LIMIT,
        name="take_rows",
    )(order, averaged)


def arrange_kernel(inverse_ref, arrived_ref, features_ref):
    tables, _, width = arrived_ref.shape
    for column in range(tables):
        features_ref[:, column * width : (column + 1) * width] = arrived_ref[inverse_ref[column]]


def arrange(arrived, inverse):
    tables, rows, width = arrived.shape
    return pl.pallas_call(
        arrange_kernel,
        out_shape=jax.ShapeDtypeStruct((rows, tables * width), arrived.dtype),
        in_specs=[smem, vmem],
        out_specs=vmem,
        compiler_params=LIMIT,
        name="arrange",
    )(inverse, arrived)


def teacher_kernel(features_ref, first, second, third, fourth, joined_ref, joined_core_ref, out_ref):
    hidden = first.shape[1]
    total = None
    for weights, joined, base in (
        (first, joined_ref, 0),
        (second, joined_ref, 2 * hidden),
        (third, joined_core_ref, 0),
        (fourth, joined_core_ref, 2 * hidden),
    ):
        held = jnp.maximum(dot(features_ref[...], weights[...]), 0.0).astype(jnp.bfloat16)
        term = dot(held, joined[base : base + hidden, :])
        term = term + dot(held, joined[base + hidden : base + 2 * hidden, :])
        total = term if total is None else total + term
    out_ref[...] = total


def teacher(features, weights, joined, joined_core):
    return pl.pallas_call(
        teacher_kernel,
        out_shape=jax.ShapeDtypeStruct((features.shape[0], joined.shape[1]), jnp.float32),
        in_specs=[vmem] * 7,
        out_specs=vmem,
        compiler_params=LIMIT,
        name="teacher",
    )(features, *weights, joined, joined_core)


def student_kernel(scale, out_ref, here_ref, there_ref, pre_ref, weights_ref, loss_ref, grads_ref):
    width = out_ref.shape[1]
    difference = out_ref[...] - (here_ref[...] + there_ref[...])
    loss_ref[...] = 0.5 * jnp.mean(difference * difference, axis=1, keepdims=True)
    out_grad = (scale * difference).astype(jnp.bfloat16)
    grads_ref[:, :width] = out_grad
    back = lax.dot_general(
        out_grad, weights_ref[...], (((1,), (1,)), ((), ())), preferred_element_type=jnp.float32
    )
    grads_ref[:, width:] = jnp.where(pre_ref[...] > 0, back, 0.0).astype(jnp.bfloat16)


def student(scale, student_out, here, there, student_pre, student_w2):
    samples, width = student_out.shape
    inner = student_pre.shape[1]
    return pl.pallas_call(
        lambda *refs: student_kernel(scale, *refs),
        out_shape=(
            jax.ShapeDtypeStruct((samples, 1), jnp.float32),
            jax.ShapeDtypeStruct((samples, width + inner), jnp.bfloat16),
        ),
        in_specs=[vmem] * 5,
        out_specs=(vmem, vmem),
        compiler_params=LIMIT,
        name="student",
    )(student_out, here, there, student_pre, student_w2)


def turn_kernel(spot_ref, own_ref, near_ref, far_ref, upper_ref, lower_ref, turned_ref):
    samples = own_ref.shape[0]
    span = own_ref.shape[1] // 2
    start = spot_ref[0] * span
    high = spot_ref[1]
    for column in range(span // 128):
        columns = pl.ds(pl.multiple_of(start + column * 128, 128), 128)
        blocks = [own_ref[:, columns], near_ref[:, columns], far_ref[:, columns]]
        blocks.append(jnp.concatenate([upper_ref[:, columns], lower_ref[:, columns]], axis=0))
        for piece, block in enumerate(blocks):
            turned = block.astype(jnp.float32).T
            for index in range(2):
                base = index * 64
                rows = jnp.where(
                    high == 0, turned[base : base + 32], turned[base + 32 : base + 64]
                ).astype(jnp.bfloat16)
                place = (2 * column + index) * 16
                for core in range(2):
                    turned_ref[
                        core, place : place + 16, piece * samples : (piece + 1) * samples
                    ] = rows[core * 16 : (core + 1) * 16]


def turn(spot, own, near, far, upper, lower):
    samples, depth = own.shape
    return pl.pallas_call(
        turn_kernel,
        out_shape=jax.ShapeDtypeStruct((2, depth // 8, 4 * samples), jnp.bfloat16),
        in_specs=[smem] + [vmem] * 5,
        out_specs=vmem,
        compiler_params=LIMIT,
        name="turn",
    )(spot, own, near, far, upper, lower)


def gradient_kernel(spot_ref, turned_ref, *refs):
    grads, hiddens, (mine_ref, other_ref) = refs[:4], refs[4:8], refs[8:]
    width = hiddens[0].shape[1]
    core = spot_ref[2]
    out_grad = jnp.concatenate([ref[:, :width] for ref in grads], axis=0)
    hidden_grad = jnp.concatenate([ref[:, width:] for ref in grads], axis=0)
    slab = pl.ds(pl.multiple_of((2 * spot_ref[0] + spot_ref[1]) * 128, 128), 128)
    hidden = jnp.concatenate([ref[:, slab] for ref in hiddens], axis=0)
    second = lax.dot_general(
        hidden, out_grad, (((0,), (0,)), ((), ())), preferred_element_type=jnp.float32
    )
    half = second.shape[0] // 2
    mine_ref[:half, :] = jnp.where(core == 0, second[:half], second[half:])
    other_ref[:half, :] = jnp.where(core == 0, second[half:], second[:half]).astype(jnp.bfloat16)
    mine_ref[half:, :] = dot(turned_ref[core], hidden_grad)
    other_ref[half:, :] = dot(turned_ref[1 - core], hidden_grad).astype(jnp.bfloat16)


def gradients(spot, turned, grads, hiddens):
    rows = turned.shape[1] + 64
    width = hiddens[0].shape[1]
    return pl.pallas_call(
        gradient_kernel,
        out_shape=(
            jax.ShapeDtypeStruct((rows, width), jnp.float32),
            jax.ShapeDtypeStruct((rows, width), jnp.bfloat16),
        ),
        in_specs=[smem] + [vmem] * 9,
        out_specs=(vmem, vmem),
        compiler_params=LIMIT,
        name="gradients",
    )(spot, turned, *grads, *hiddens)


def assemble_kernel(spot_ref, own_ref, near_ref, far_ref, opposite_ref, core_ref, out_ref):
    rows = own_ref.shape[0]
    group, high, core = spot_ref[0], spot_ref[1], spot_ref[2]
    for index, (ref, at) in enumerate(
        (
            (own_ref, 2 * group + high),
            (near_ref, 2 * (1 - group) + high),
            (far_ref, 2 * (1 - group) + 1 - high),
            (opposite_ref, 2 * group + 1 - high),
        )
    ):
        here = pl.multiple_of((2 * at + core) * rows, rows)
        there = pl.multiple_of((2 * at + 1 - core) * rows, rows)
        out_ref[pl.ds(here, rows), :] = ref[...]
        out_ref[pl.ds(there, rows), :] = core_ref[index * rows : (index + 1) * rows, :]


def assemble(spot, own, near, far, opposite, core):
    return pl.pallas_call(
        assemble_kernel,
        out_shape=jax.ShapeDtypeStruct((8 * own.shape[0], own.shape[1]), jnp.float32),
        in_specs=[smem] + [vmem] * 5,
        out_specs=vmem,
        compiler_params=LIMIT,
        name="assemble",
    )(spot, own, near, far, opposite, core)


def shards(
    pooled,
    counts,
    sample_order,
    table_order,
    teacher_w1,
    teacher_w2,
    projection,
    student_w1,
    student_w2,
):
    group = lax.axis_index("grp")
    member = lax.axis_index("mp")
    spot = jnp.stack([group, member // 2, member % 2]).astype(jnp.int32)
    tables = table_order.shape[0]
    block, width = pooled.shape[2:]
    samples = block // tables
    inner, outer = student_w2.shape

    near_w1 = swap(teacher_w1, NEAR)
    joined = split_two(dot(teacher_w2, projection))
    joined = jnp.concatenate([joined, swap(joined, NEAR)], axis=0)
    joined_core = swap(joined, CORE)
    weights = (teacher_w1, near_w1, swap(teacher_w1, CORE), swap(near_w1, CORE))

    table_range = jnp.arange(tables, dtype=jnp.int32)
    inverse = jnp.sum(
        jnp.where(table_order[None, :] == table_range[:, None], table_range[None, :], 0), axis=1
    )
    divisor = jnp.maximum(counts[0, 0], 1).astype(jnp.float32)
    averaged = pooled[0, 0].astype(jnp.float32) / divisor[:, None]
    ordered = take_rows(averaged, sample_order)
    arrived = lax.all_to_all(
        ordered.reshape(tables, samples, width), "dp", split_axis=0, concat_axis=0, tiled=True
    )
    own = arrange(arrived, inverse)
    far = swap(own, FAR)
    near = swap(own, NEAR)

    there = swap(teacher(far, weights, joined, joined_core), FAR)
    here = teacher(own, weights, joined, joined_core)

    student_pre = dot(own, student_w1)
    student_hidden = jax.nn.relu(student_pre).astype(jnp.bfloat16)
    student_out = dot(student_hidden, student_w2)
    hiddens = [student_hidden] + [swap(student_hidden, mask) for mask in (NEAR, FAR, OPPOSITE)]

    devices = lax.axis_size("grp") * lax.axis_size("dp") * lax.axis_size("mp")
    grad_scale = 8192.0 / (samples * devices * outer)
    sample_loss, grads = student(grad_scale, student_out, here, there, student_pre, student_w2)
    grads = [grads] + [swap(grads, mask) for mask in (NEAR, FAR, OPPOSITE)]

    upper = swap(near[: samples // 2], FAR)
    lower = swap(far[samples // 2 :], NEAR)
    turned = turn(spot, own, near, far, upper, lower)

    mine, other = gradients(spot, turned, grads, hiddens)
    mine = mine + swap(other, CORE).astype(jnp.float32)
    slab = inner // 8
    second = lax.all_to_all(
        mine[:slab].reshape(tables, slab // tables, outer),
        "dp",
        split_axis=0,
        concat_axis=0,
        tiled=True,
    )
    first = lax.all_to_all(
        mine[slab:].astype(jnp.bfloat16).reshape(tables, -1, inner),
        "dp",
        split_axis=0,
        concat_axis=0,
        tiled=True,
    )
    grad_w1 = jnp.sum(first.astype(jnp.float32), axis=0)
    second = jnp.sum(second, axis=0)
    second = lax.all_to_all(
        jnp.broadcast_to(second[None], (tables,) + second.shape),
        "dp",
        split_axis=0,
        concat_axis=0,
        tiled=True,
    ).reshape(slab, outer)
    seconds = [second] + [swap(second, mask) for mask in (NEAR, FAR, OPPOSITE)]
    grad_w2 = assemble(spot, *seconds, swap(jnp.concatenate(seconds, axis=0), CORE))
    return (grad_w1, grad_w2, sample_loss.reshape(1, samples))


def solution(mesh):
    return jax.shard_map(
        shards,
        mesh=mesh,
        in_specs=(
            P("dp", LINE, None, None),
            P("dp", LINE, None),
            P(LINE, None),
            P(),
            P(None, LINE),
            P(LINE, None),
            P(),
            P(),
            P(),
        ),
        out_specs=(P(("grp", "dp", "mp"), None), P(), P(LINE, "dp")),
        check_vma=False,
    )
```

time: 1850 us -> 196 us (0.11)
  waiting for transfers between devices: 1740 us -> 84.1 us
  starting transfers between devices: 11.5 us -> 42.8 us
  matrix products: 26.6 us -> 2.87 us
  Pallas kernels: 0 us -> 22.3 us
  blocking collectives: 0 us -> 21.5 us
  local copies, waits for them, and re-layouts: 31.7 us -> 12.1 us
    reduce_scatter x2 -> x0, waiting for transfers between devices: 1370 us -> none  [the longest x1 1280 us: shards(): lax.psum_scatter(contract_rows(features, hidden_grad), ('grp', 'dp', 'mp'...]
    psum x1 -> x0, waiting for transfers between devices: 247 us -> none  [shards(): lax.psum(contract_rows(student_hidden, out_grad), ('grp', 'dp', 'mp'))]
    all_gather x1 -> x0, waiting for transfers between devices: 97.1 us -> none  [shards(): lax.all_gather(features, ('grp', 'mp'), axis=0, tiled=True)]
    ppermute x0 -> x21, waiting for transfers between devices: none -> 70.6 us  [swap(): lax.ppermute(values, LINE, [(index, index ^ mask) for index in range(8)])]
    dot_general x8 -> x3, matrix products: 26.6 us -> 2.87 us  [dot(): return jnp.dot(left, right, preferred_element_type=jnp.float32)]
    pallas_call x0 -> x8, Pallas kernels: none -> 22.3 us  [the longest x2 10.9 us: teacher(): pl.pallas_call(teacher_kernel, out_shape=jax.ShapeDtypeStruct((features.s...]
    ppermute x0 -> x21, starting transfers between devices: none -> 22 us  [swap(): lax.ppermute(values, LINE, [(index, index ^ mask) for index in range(8)])]
    all_to_all x0 -> x1, blocking collectives: none -> 21.5 us  [shards(): lax.all_to_all(mine[:slab].reshape(tables, slab // tables, outer), 'dp',...]
  transfers between devices with their start and end apart: 5 -> 24, of which waited for: 5 -> 12; matrix products, arithmetic and copies ran while one was open for 1% -> 6% of each run, Pallas kernels for 0% -> 10%
where the time goes in v1:
time: 196 us; the launch traced here: 195 us
  waiting for transfers between devices  84.1 us (43%)
  starting transfers between devices  42.8 us (22%)
  Pallas kernels  22.3 us (11%)
  blocking collectives  21.5 us (11%)
  local copies, waits for them, and re-layouts  12.1 us (6%)
  other arithmetic  8.21 us (4%)
  matrix products  2.87 us (1%)
    ppermute x21, waiting for transfers between devices, swap(): lax.ppermute(values, LINE, [(index, index ^ mask) for index in range(8)])  70.6 us
    ppermute x21, starting transfers between devices, swap(): lax.ppermute(values, LINE, [(index, index ^ mask) for index in range(8)])  22 us
    all_to_all x1, blocking collectives, shards(): lax.all_to_all(mine[:slab].reshape(tables, slab // tables, outer), 'dp',...  21.5 us
    all_to_all x1, starting transfers between devices, shards(): lax.all_to_all(ordered.reshape(tables, samples, width), 'dp', split_axis=...  11.4 us
    pallas_call x2, Pallas kernels, teacher(): pl.pallas_call(teacher_kernel, out_shape=jax.ShapeDtypeStruct((features.s...  10.9 us
    unnamed x44, local copies, waits for them, and re-layouts  9.64 us
    all_to_all x1, waiting for transfers between devices, shards(): lax.all_to_all(jnp.broadcast_to(second[None], (tables,) + second.shape),...  8.99 us
    pallas_call x1, Pallas kernels, take_rows(): pl.pallas_call(order_kernel, out_shape=jax.ShapeDtypeStruct(averaged.shap...  5.48 us
  transfers between devices with their start and end apart: 24, of which 12 were waited for; matrix products, arithmetic and copies ran while one was open for 6% of the time, Pallas kernels for 10%

profile of v1, /device:TPU:32, one launch (start us, length us, event | category | flops | bytes accessed | tf_op | source)
XLA Modules:
  0.0 194.8 jit_solution(16686678685588225231)
XLA Ops:
  4.8 5.5 %take_rows.1 = bf16[4096,128]{1,0:T(8,128)(2,1)} custom-call(s32[1,4096]{1,0:T(1,128)S(1)} %copy-done.17, f32[4096,128]{1,0:T(8,128)S(1)} %convert_divide_fusion.averaged_ref), custom_call_target="tpu_custom_call" | custom-call | tf_op jit(solution)/shard_map/take_rows/pallas_call | solution.py:41
  10.2 11.4 %all-to-all-start = ((bf16[32,128,128]{2,1,0:T(8,128)(2,1)}), bf16[32,128,128]{2,1,0:T(8,128)(2,1)S(1)}, u32[]{:S(2)}, u32[]{:S(2)}) async-start(bf16[32,128,128]{2,1,0:T(8,128)(2,1)} %bitcast.5), calls=%async_computation | async-start | bytes 2097152 | tf_op jit(solution)/shard_map/all_to_all | solution.py:253
  21.7 26.7 %collective-permute-done.4.second = bf16[4096,256]{1,0:T(8,128)(2,1)} collective-permute-done((bf16[4096,256]{1,0:T(8,128)(2,1)}, bf16[4096,256]{1,0:T(8,128)(2,1)}, u32[]{:S(2)}, u32[]{:S(2)}) %collective-permute-start.4) | collective-permute-done | bytes 2097184 | tf_op jit(solution)/shard_map/ppermute | solution.py:21
  48.4 1.9 fusion
  56.0 2.2 %collective-permute-start.1 = (bf16[128,4096]{1,0:T(8,128)(2,1)S(1)}, bf16[128,4096]{1,0:T(8,128)(2,1)S(1)}, u32[]{:S(2)}, u32[]{:S(2)}) collective-permute-start(bf16[128,4096]{1,0:T(8,128)(2,1)S(1)} %arrange.1.own_ref.features_ref), channel_id=1, source_target_pairs={{0,130},{1,131},{2,128},{3,129},{128,2},{129,3},{130,0},{131,1},{4... | collective-permute-start | bytes 3145736 | tf_op jit(solution)/shard_map/ppermute | solution.py:21
  58.8 7.6 %collective-permute-done.7 = bf16[512,512]{1,0:T(8,128)(2,1)} collective-permute-done((bf16[512,512]{1,0:T(8,128)(2,1)}, bf16[512,512]{1,0:T(8,128)(2,1)}, u32[]{:S(2)}, u32[]{:S(2)}) %collective-permute-start.7) | collective-permute-done | bytes 524320 | tf_op jit(solution)/shard_map/ppermute | solution.py:21
  67.6 15.0 %collective-permute-done.1.far_ref.features_ref = bf16[128,4096]{1,0:T(8,128)(2,1)S(1)} collective-permute-done((bf16[128,4096]{1,0:T(8,128)(2,1)S(1)}, bf16[128,4096]{1,0:T(8,128)(2,1)S(1)}, u32[]{:S(2)}, u32[]{:S(2)}) %collective-permute-start.1) | collective-permute-done | bytes 1048608 | tf_op jit(solution)/shard_map/ppermute | solution.py:21
  82.7 6.0 %collective-permute-done.near_ref = bf16[128,4096]{1,0:T(8,128)(2,1)S(1)} collective-permute-done((bf16[128,4096]{1,0:T(8,128)(2,1)S(1)}, bf16[128,4096]{1,0:T(8,128)(2,1)S(1)}, u32[]{:S(2)}, u32[]{:S(2)}) %collective-permute-start) | collective-permute-done | bytes 1048608 | tf_op jit(solution)/shard_map/ppermute | solution.py:21
  88.8 2.8 %collective-permute-start.2 = (bf16[64,4096]{1,0:T(8,128)(2,1)S(1)}, bf16[64,4096]{1,0:T(8,128)(2,1)S(1)}, u32[]{:S(2)}, u32[]{:S(2)}) collective-permute-start(bf16[64,4096]{1,0:T(8,128)(2,1)S(1)} %slice.17), channel_id=1, source_target_pairs={{0,130},{1,131},{2,128},{3,129},{128,2},{129,3},{130,0},{131,1},{4... | collective-permute-start | bytes 1572872 | tf_op jit(solution)/shard_map/ppermute | solution.py:21
  91.7 5.4 %teacher.3 = f32[128,512]{1,0:T(8,128)S(1)} custom-call(bf16[128,4096]{1,0:T(8,128)(2,1)S(1)} %collective-permute-done.1.far_ref.features_ref, bf16[4096,256]{1,0:T(8,128)(2,1)S(1)} %copy-done.1, bf16[4096,256]{1,0:T(8,128)(2,1)} %collective-permute-done.4.second, bf16[4096,256]{1,0:T(8,128)(2,1)} %collective-permute-done.5.third, ...), custom_call_target="tpu_custom_call" | custom-call | tf_op jit(solution)/shard_map/teacher/pallas_call | solution.py:86
  99.9 5.4 %teacher.2.refs_1_ = f32[128,512]{1,0:T(8,128)S(1)} custom-call(bf16[128,4096]{1,0:T(8,128)(2,1)S(1)} %arrange.1.own_ref.features_ref, bf16[4096,256]{1,0:T(8,128)(2,1)S(1)} %copy-done.1, bf16[4096,256]{1,0:T(8,128)(2,1)} %collective-permute-done.4.second, bf16[4096,256]{1,0:T(8,128)(2,1)} %collective-permute-done.5.third, ...), custom_call_target="tpu_custom_call" | custom-call | tf_op jit(solution)/shard_map/teacher/pallas_call | solution.py:86
  105.3 3.5 %collective-permute-done.9.refs_2_ = f32[128,512]{1,0:T(8,128)S(1)} collective-permute-done((f32[128,512]{1,0:T(8,128)S(1)}, f32[128,512]{1,0:T(8,128)S(1)}, u32[]{:S(2)}, u32[]{:S(2)}) %collective-permute-start.9) | collective-permute-done | bytes 262176 | tf_op jit(solution)/shard_map/ppermute | solution.py:21
  110.1 2.5 %collective-permute-start.11 = (bf16[128,1024]{1,0:T(8,128)(2,1)S(1)}, bf16[128,1024]{1,0:T(8,128)(2,1)}, u32[]{:S(2)}, u32[]{:S(2)}) collective-permute-start(bf16[128,1024]{1,0:T(8,128)(2,1)S(1)} %get-tuple-element.7.refs_0_), channel_id=1, source_target_pairs={{0,130},{1,131},{2,128},{3,129},{128,2},{129,3},{130,0},{131,1},{4... | collective-permute-start | bytes 786440 | tf_op jit(solution)/shard_map/ppermute | solution.py:21
  115.5 2.6 %collective-permute-start.14 = (bf16[128,512]{1,0:T(8,128)(2,1)S(1)}, bf16[128,512]{1,0:T(8,128)(2,1)}, u32[]{:S(2)}, u32[]{:S(2)}) collective-permute-start(bf16[128,512]{1,0:T(8,128)(2,1)S(1)} %get-tuple-element.11.refs_4_), channel_id=1, source_target_pairs={{0,130},{1,131},{2,128},{3,129},{128,2},{129,3},{130,0},{131,1},{4... | collective-permute-start | bytes 393224 | tf_op jit(solution)/shard_map/ppermute | solution.py:21
  124.8 4.2 %collective-permute-done.14.refs_6_ = bf16[128,512]{1,0:T(8,128)(2,1)} collective-permute-done((bf16[128,512]{1,0:T(8,128)(2,1)S(1)}, bf16[128,512]{1,0:T(8,128)(2,1)}, u32[]{:S(2)}, u32[]{:S(2)}) %collective-permute-start.14) | collective-permute-done | bytes 131104 | tf_op jit(solution)/shard_map/ppermute | solution.py:21
  129.0 2.0 %gradients.1 = (f32[576,512]{1,0:T(8,128)S(1)}, bf16[576,512]{1,0:T(8,128)(2,1)S(1)}) custom-call(s32[3]{0:T(128)S(1)} %pad_add_fusion.spot_ref, bf16[2,512,512]{2,1,0:T(8,128)(2,1)S(1)} %turn.1.turned_ref, bf16[128,1024]{1,0:T(8,128)(2,1)S(1)} %get-tuple-element.7.refs_0_, bf16[128,1024]{1,0:T(8,128)(2,1)} %collective-permute-done.10.refs_1_, ...), custom_call_target="tpu_custom_call" | custom-call | tf_op jit(solution)/shard_map/gradients/pallas_call | solution.py:180
  131.2 2.0 %collective-permute-done.16 = bf16[576,512]{1,0:T(8,128)(2,1)S(1)} collective-permute-done((bf16[576,512]{1,0:T(8,128)(2,1)S(1)}, bf16[576,512]{1,0:T(8,128)(2,1)S(1)}, u32[]{:S(2)}, u32[]{:S(2)}) %collective-permute-start.16) | collective-permute-done | bytes 589856 | tf_op jit(solution)/shard_map/ppermute | solution.py:21
  134.1 21.5 %all_to_all.20 = f32[32,2,512]{2,1,0:T(2,128)S(1)} all-to-all(f32[32,2,512]{2,1,0:T(2,128)} %reshape.36), channel_id=1, replica_groups=mesh['grp'=2,'dp'=32,'mp'=4] {'dp'}, dimensions={0} | all-to-all | bytes 262144 | tf_op jit(solution)/shard_map/all_to_all | solution.py:280
  156.3 4.3 %all-to-all-start.3 = ((f32[32,2,512]{2,1,0:T(2,128)}), f32[32,2,512]{2,1,0:T(2,128)S(1)}, u32[]{:S(2)}, u32[]{:S(2)}) async-start(f32[32,2,512]{2,1,0:T(2,128)} %broadcast_in_dim.24), calls=%async_computation.3 | async-start | bytes 262144 | tf_op jit(solution)/shard_map/all_to_all | solution.py:296
  161.6 9.0 %all-to-all-done.3 = f32[32,2,512]{2,1,0:T(2,128)S(1)} async-done(((f32[32,2,512]{2,1,0:T(2,128)}), f32[32,2,512]{2,1,0:T(2,128)S(1)}, u32[]{:S(2)}, u32[]{:S(2)}) %all-to-all-start.3) | async-done | bytes 131104 | tf_op jit(solution)/shard_map/all_to_all | solution.py:296
  170.5 5.1 %all-to-all-start.1 = ((bf16[32,16,512]{2,1,0:T(8,128)(2,1)}), bf16[32,16,512]{2,1,0:T(8,128)(2,1)}, u32[]{:S(2)}, u32[]{:S(2)}) async-start(bf16[32,16,512]{2,1,0:T(8,128)(2,1)} %bitcast.16), calls=%async_computation.1 | async-start | bytes 1048576 | tf_op jit(solution)/shard_map/all_to_all | solution.py:287
  176.8 2.3 %collective-permute-start.18 = (f32[64,512]{1,0:T(8,128)S(1)}, f32[64,512]{1,0:T(8,128)S(1)}, u32[]{:S(2)}, u32[]{:S(2)}) collective-permute-start(f32[64,512]{1,0:T(8,128)S(1)} %reshape.37.own_ref), channel_id=1, source_target_pairs={{0,130},{1,131},{2,128},{3,129},{128,2},{129,3},{130,0},{131,1},{4... | collective-permute-start | bytes 393224 | tf_op jit(solution)/shard_map/ppermute | solution.py:21
  183.0 2.6 %collective-permute-done.19.opposite_ref = f32[64,512]{1,0:T(8,128)S(1)} collective-permute-done((f32[64,512]{1,0:T(8,128)S(1)}, f32[64,512]{1,0:T(8,128)S(1)}, u32[]{:S(2)}, u32[]{:S(2)}) %collective-permute-start.19) | collective-permute-done | bytes 131104 | tf_op jit(solution)/shard_map/ppermute | solution.py:21
  187.1 4.4 %all-to-all-done.1 = bf16[32,16,512]{2,1,0:T(8,128)(2,1)} async-done(((bf16[32,16,512]{2,1,0:T(8,128)(2,1)}), bf16[32,16,512]{2,1,0:T(8,128)(2,1)}, u32[]{:S(2)}, u32[]{:S(2)}) %all-to-all-start.1) | async-done | bytes 524320 | tf_op jit(solution)/shard_map/all_to_all | solution.py:287
  (99 shorter events, 37.6 us)
Async XLA Ops:
  0.7 47.8 %collective-permute-start.4 = (bf16[4096,256]{1,0:T(8,128)(2,1)}, bf16[4096,256]{1,0:T(8,128)(2,1)}, u32[]{:S(2)}, u32[]{:S(2)}) collective-permute-start(bf16[4096,256]{1,0:T(8,128)(2,1)} %first.3), channel_id=1, source_target_pairs={{0,128},{1,129},{2,130},{3,131},{128,0},{129,1},{130,2},{131,3},{4... | collective-permute-start | bytes 6291464 | tf_op jit(solution)/shard_map/ppermute | solution.py:21
  10.2 42.7 %all-to-all-start = ((bf16[32,128,128]{2,1,0:T(8,128)(2,1)}), bf16[32,128,128]{2,1,0:T(8,128)(2,1)S(1)}, u32[]{:S(2)}, u32[]{:S(2)}) async-start(bf16[32,128,128]{2,1,0:T(8,128)(2,1)} %bitcast.5), calls=%async_computation | async-start | bytes 2097152 | tf_op jit(solution)/shard_map/all_to_all | solution.py:253
  21.6 70.0 %collective-permute-start.5 = (bf16[4096,256]{1,0:T(8,128)(2,1)}, bf16[4096,256]{1,0:T(8,128)(2,1)}, u32[]{:S(2)}, u32[]{:S(2)}) collective-permute-start(bf16[4096,256]{1,0:T(8,128)(2,1)} %first.3), channel_id=1, source_target_pairs={{0,1},{1,0},{2,3},{3,2},{128,129},{129,128},{130,131},{131,130},{4... | collective-permute-start | bytes 6291464 | tf_op jit(solution)/shard_map/ppermute | solution.py:21
  48.4 43.2 %collective-permute-start.6 = (bf16[4096,256]{1,0:T(8,128)(2,1)}, bf16[4096,256]{1,0:T(8,128)(2,1)}, u32[]{:S(2)}, u32[]{:S(2)}) collective-permute-start(bf16[4096,256]{1,0:T(8,128)(2,1)} %collective-permute-done.4.second), channel_id=1, source_target_pairs={{0,1},{1,0},{2,3},{3,2},{128,129},{129,128},{130,131},{131,130},{4... | collective-permute-start | bytes 6291464 | tf_op jit(solution)/shard_map/ppermute | solution.py:21
  51.3 15.0 %collective-permute-start.7 = (bf16[512,512]{1,0:T(8,128)(2,1)}, bf16[512,512]{1,0:T(8,128)(2,1)}, u32[]{:S(2)}, u32[]{:S(2)}) collective-permute-start(bf16[512,512]{1,0:T(8,128)(2,1)} %pad_maximum_fusion.1), channel_id=1, source_target_pairs={{0,128},{1,129},{2,130},{3,131},{128,0},{129,1},{130,2},{131,3},{4... | collective-permute-start | bytes 1572872 | tf_op jit(solution)/shard_map/ppermute | solution.py:21
  56.0 26.6 %collective-permute-start.1 = (bf16[128,4096]{1,0:T(8,128)(2,1)S(1)}, bf16[128,4096]{1,0:T(8,128)(2,1)S(1)}, u32[]{:S(2)}, u32[]{:S(2)}) collective-permute-start(bf16[128,4096]{1,0:T(8,128)(2,1)S(1)} %arrange.1.own_ref.features_ref), channel_id=1, source_target_pairs={{0,130},{1,131},{2,128},{3,129},{128,2},{129,3},{130,0},{131,1},{4... | collective-permute-start | bytes 3145736 | tf_op jit(solution)/shard_map/ppermute | solution.py:21
  58.2 30.6 %collective-permute-start = (bf16[128,4096]{1,0:T(8,128)(2,1)S(1)}, bf16[128,4096]{1,0:T(8,128)(2,1)S(1)}, u32[]{:S(2)}, u32[]{:S(2)}) collective-permute-start(bf16[128,4096]{1,0:T(8,128)(2,1)S(1)} %arrange.1.own_ref.features_ref), channel_id=1, source_target_pairs={{0,128},{1,129},{2,130},{3,131},{128,0},{129,1},{130,2},{131,3},{4... | collective-permute-start | bytes 3145736 | tf_op jit(solution)/shard_map/ppermute | solution.py:21
  67.5 24.2 %collective-permute-start.8 = (bf16[1024,512]{1,0:T(8,128)(2,1)S(1)}, bf16[1024,512]{1,0:T(8,128)(2,1)S(1)}, u32[]{:S(2)}, u32[]{:S(2)}) collective-permute-start(bf16[1024,512]{1,0:T(8,128)(2,1)S(1)} %pad_maximum_fusion.joined_ref), channel_id=1, source_target_pairs={{0,1},{1,0},{2,3},{3,2},{128,129},{129,128},{130,131},{131,130},{4... | collective-permute-start | bytes 3145736 | tf_op jit(solution)/shard_map/ppermute | solution.py:21
  82.6 32.1 %collective-permute-start.3 = (bf16[64,4096]{1,0:T(8,128)(2,1)S(1)}, bf16[64,4096]{1,0:T(8,128)(2,1)S(1)}, u32[]{:S(2)}, u32[]{:S(2)}) collective-permute-start(bf16[64,4096]{1,0:T(8,128)(2,1)S(1)} %slice.18), channel_id=1, source_target_pairs={{0,128},{1,129},{2,130},{3,131},{128,0},{129,1},{130,2},{131,3},{4... | collective-permute-start | bytes 1572872 | tf_op jit(solution)/shard_map/ppermute | solution.py:21
  88.8 29.3 %collective-permute-start.2 = (bf16[64,4096]{1,0:T(8,128)(2,1)S(1)}, bf16[64,4096]{1,0:T(8,128)(2,1)S(1)}, u32[]{:S(2)}, u32[]{:S(2)}) collective-permute-start(bf16[64,4096]{1,0:T(8,128)(2,1)S(1)} %slice.17), channel_id=1, source_target_pairs={{0,130},{1,131},{2,128},{3,129},{128,2},{129,3},{130,0},{131,1},{4... | collective-permute-start | bytes 1572872 | tf_op jit(solution)/shard_map/ppermute | solution.py:21
  97.1 11.7 %collective-permute-start.9 = (f32[128,512]{1,0:T(8,128)S(1)}, f32[128,512]{1,0:T(8,128)S(1)}, u32[]{:S(2)}, u32[]{:S(2)}) collective-permute-start(f32[128,512]{1,0:T(8,128)S(1)} %teacher.3), channel_id=1, source_target_pairs={{0,130},{1,131},{2,128},{3,129},{128,2},{129,3},{130,0},{131,1},{4... | collective-permute-start | bytes 786440 | tf_op jit(solution)/shard_map/ppermute | solution.py:21
  99.1 13.5 %collective-permute-start.13 = (bf16[128,512]{1,0:T(8,128)(2,1)S(1)}, bf16[128,512]{1,0:T(8,128)(2,1)S(1)}, u32[]{:S(2)}, u32[]{:S(2)}) collective-permute-start(bf16[128,512]{1,0:T(8,128)(2,1)S(1)} %get-tuple-element.11.refs_4_), channel_id=1, source_target_pairs={{0,128},{1,129},{2,130},{3,131},{128,0},{129,1},{130,2},{131,3},{4... | collective-permute-start | bytes 393224 | tf_op jit(solution)/shard_map/ppermute | solution.py:21
  109.8 19.2 %collective-permute-start.10 = (bf16[128,1024]{1,0:T(8,128)(2,1)S(1)}, bf16[128,1024]{1,0:T(8,128)(2,1)}, u32[]{:S(2)}, u32[]{:S(2)}) collective-permute-start(bf16[128,1024]{1,0:T(8,128)(2,1)S(1)} %get-tuple-element.7.refs_0_), channel_id=1, source_target_pairs={{0,128},{1,129},{2,130},{3,131},{128,0},{129,1},{130,2},{131,3},{4... | collective-permute-start | bytes 786440 | tf_op jit(solution)/shard_map/ppermute | solution.py:21
  110.1 18.9 %collective-permute-start.11 = (bf16[128,1024]{1,0:T(8,128)(2,1)S(1)}, bf16[128,1024]{1,0:T(8,128)(2,1)}, u32[]{:S(2)}, u32[]{:S(2)}) collective-permute-start(bf16[128,1024]{1,0:T(8,128)(2,1)S(1)} %get-tuple-element.7.refs_0_), channel_id=1, source_target_pairs={{0,130},{1,131},{2,128},{3,129},{128,2},{129,3},{130,0},{131,1},{4... | collective-permute-start | bytes 786440 | tf_op jit(solution)/shard_map/ppermute | solution.py:21
  113.2 15.8 %collective-permute-start.12 = (bf16[128,1024]{1,0:T(8,128)(2,1)S(1)}, bf16[128,1024]{1,0:T(8,128)(2,1)}, u32[]{:S(2)}, u32[]{:S(2)}) collective-permute-start(bf16[128,1024]{1,0:T(8,128)(2,1)S(1)} %get-tuple-element.7.refs_0_), channel_id=1, source_target_pairs={{0,2},{1,3},{2,0},{3,1},{128,130},{129,131},{130,128},{131,129},{4... | collective-permute-start | bytes 786440 | tf_op jit(solution)/shard_map/ppermute | solution.py:21
  115.5 13.5 %collective-permute-start.14 = (bf16[128,512]{1,0:T(8,128)(2,1)S(1)}, bf16[128,512]{1,0:T(8,128)(2,1)}, u32[]{:S(2)}, u32[]{:S(2)}) collective-permute-start(bf16[128,512]{1,0:T(8,128)(2,1)S(1)} %get-tuple-element.11.refs_4_), channel_id=1, source_target_pairs={{0,130},{1,131},{2,128},{3,129},{128,2},{129,3},{130,0},{131,1},{4... | collective-permute-start | bytes 393224 | tf_op jit(solution)/shard_map/ppermute | solution.py:21
  118.9 10.1 %collective-permute-start.15 = (bf16[128,512]{1,0:T(8,128)(2,1)S(1)}, bf16[128,512]{1,0:T(8,128)(2,1)}, u32[]{:S(2)}, u32[]{:S(2)}) collective-permute-start(bf16[128,512]{1,0:T(8,128)(2,1)S(1)} %get-tuple-element.11.refs_4_), channel_id=1, source_target_pairs={{0,2},{1,3},{2,0},{3,1},{128,130},{129,131},{130,128},{131,129},{4... | collective-permute-start | bytes 393224 | tf_op jit(solution)/shard_map/ppermute | solution.py:21
  131.1 2.1 %collective-permute-start.16 = (bf16[576,512]{1,0:T(8,128)(2,1)S(1)}, bf16[576,512]{1,0:T(8,128)(2,1)S(1)}, u32[]{:S(2)}, u32[]{:S(2)}) collective-permute-start(bf16[576,512]{1,0:T(8,128)(2,1)S(1)} %get-tuple-element.9), channel_id=1, source_target_pairs={{0,1},{1,0},{2,3},{3,2},{128,129},{129,128},{130,131},{131,130},{4... | collective-permute-start | bytes 1769480 | tf_op jit(solution)/shard_map/ppermute | solution.py:21
  156.3 14.2 %all-to-all-start.3 = ((f32[32,2,512]{2,1,0:T(2,128)}), f32[32,2,512]{2,1,0:T(2,128)S(1)}, u32[]{:S(2)}, u32[]{:S(2)}) async-start(f32[32,2,512]{2,1,0:T(2,128)} %broadcast_in_dim.24), calls=%async_computation.3 | async-start | bytes 262144 | tf_op jit(solution)/shard_map/all_to_all | solution.py:296
  170.5 21.0 %all-to-all-start.1 = ((bf16[32,16,512]{2,1,0:T(8,128)(2,1)}), bf16[32,16,512]{2,1,0:T(8,128)(2,1)}, u32[]{:S(2)}, u32[]{:S(2)}) async-start(bf16[32,16,512]{2,1,0:T(8,128)(2,1)} %bitcast.16), calls=%async_computation.1 | async-start | bytes 1048576 | tf_op jit(solution)/shard_map/all_to_all | solution.py:287
  175.8 5.3 %collective-permute-start.17 = (f32[64,512]{1,0:T(8,128)S(1)}, f32[64,512]{1,0:T(8,128)S(1)}, u32[]{:S(2)}, u32[]{:S(2)}) collective-permute-start(f32[64,512]{1,0:T(8,128)S(1)} %reshape.37.own_ref), channel_id=1, source_target_pairs={{0,128},{1,129},{2,130},{3,131},{128,0},{129,1},{130,2},{131,3},{4... | collective-permute-start | bytes 393224 | tf_op jit(solution)/shard_map/ppermute | solution.py:21
  176.8 6.2 %collective-permute-start.18 = (f32[64,512]{1,0:T(8,128)S(1)}, f32[64,512]{1,0:T(8,128)S(1)}, u32[]{:S(2)}, u32[]{:S(2)}) collective-permute-start(f32[64,512]{1,0:T(8,128)S(1)} %reshape.37.own_ref), channel_id=1, source_target_pairs={{0,130},{1,131},{2,128},{3,129},{128,2},{129,3},{130,0},{131,1},{4... | collective-permute-start | bytes 393224 | tf_op jit(solution)/shard_map/ppermute | solution.py:21
  179.1 6.5 %collective-permute-start.19 = (f32[64,512]{1,0:T(8,128)S(1)}, f32[64,512]{1,0:T(8,128)S(1)}, u32[]{:S(2)}, u32[]{:S(2)}) collective-permute-start(f32[64,512]{1,0:T(8,128)S(1)} %reshape.37.own_ref), channel_id=1, source_target_pairs={{0,2},{1,3},{2,0},{3,1},{128,130},{129,131},{130,128},{131,129},{4... | collective-permute-start | bytes 393224 | tf_op jit(solution)/shard_map/ppermute | solution.py:21
  186.5 6.8 %collective-permute-start.20 = (f32[256,512]{1,0:T(8,128)}, f32[256,512]{1,0:T(8,128)S(1)}, u32[]{:S(2)}, u32[]{:S(2)}) collective-permute-start(f32[256,512]{1,0:T(8,128)} %pad_maximum_fusion.2), channel_id=1, source_target_pairs={{0,1},{1,0},{2,3},{3,2},{128,129},{129,128},{130,131},{131,130},{4... | collective-permute-start | bytes 1572872 | tf_op jit(solution)/shard_map/ppermute | solution.py:21
  (22 other events, 234.9 us)

commit v2 on v1

v2 whole, which is shorter than its diff:
```python
import jax
import jax.numpy as jnp
from jax import lax
from jax.experimental import pallas as pl
from jax.experimental.pallas import tpu as pltpu
from jax.sharding import PartitionSpec as P

LINE = ("grp", "mp")
CORE, NEAR, FAR, OPPOSITE = 1, 4, 6, 2

smem = pl.BlockSpec(memory_space=pltpu.SMEM)
vmem = pl.BlockSpec(memory_space=pltpu.VMEM)
anywhere = pl.BlockSpec(memory_space=pl.ANY)


def limit(mebibytes):
    return pltpu.CompilerParams(vmem_limit_bytes=mebibytes * 1024 * 1024)


def tie(*values):
    return lax.optimization_barrier(values)


def dot(left, right):
    return jnp.dot(left, right, preferred_element_type=jnp.float32)


def swap(values, mask):
    return lax.ppermute(values, LINE, [(index, index ^ mask) for index in range(8)])


def split_two(values):
    upper = lax.optimization_barrier(values.astype(jnp.bfloat16))
    lower = (values - upper.astype(jnp.float32)).astype(jnp.bfloat16)
    return jnp.concatenate([upper, lower], axis=0)


def across(values):
    return lax.all_to_all(values, "dp", split_axis=0, concat_axis=0, tiled=True)


def total_of(values, parts):
    return jnp.sum(values.reshape(parts, -1, values.shape[1]).astype(jnp.float32), axis=0)


def order_kernel(order_ref, averaged_ref, ordered_ref):
    step = 64

    @pl.loop(0, ordered_ref.shape[0] // step)
    def _(index):
        base = pl.multiple_of(index * step, step)
        rows = [averaged_ref[pl.ds(order_ref[0, base + row], 1), :] for row in range(step)]
        ordered_ref[pl.ds(base, step), :] = jnp.concatenate(rows, axis=0).astype(jnp.bfloat16)


def take_rows(averaged, order):
    return pl.pallas_call(
        order_kernel,
        out_shape=jax.ShapeDtypeStruct(averaged.shape, jnp.bfloat16),
        in_specs=[smem, vmem],
        out_specs=vmem,
        compiler_params=limit(8),
        name="take_rows",
    )(order, averaged)


def arrange_kernel(inverse_ref, arrived_ref, features_ref, semaphores):
    tables, _, width = arrived_ref.shape
    copies = [
        pltpu.make_async_copy(
            arrived_ref.at[inverse_ref[column]],
            features_ref.at[:, column * width : (column + 1) * width],
            semaphores.at[column],
        )
        for column in range(tables)
    ]
    for copy in copies:
        copy.start()
    for copy in copies:
        copy.wait()


def arrange(arrived, inverse):
    tables, rows, width = arrived.shape
    return pl.pallas_call(
        arrange_kernel,
        out_shape=jax.ShapeDtypeStruct((rows, tables * width), arrived.dtype),
        in_specs=[smem, pl.BlockSpec(memory_space=pltpu.HBM)],
        out_specs=vmem,
        scratch_shapes=[pltpu.SemaphoreType.DMA((tables,))],
        compiler_params=limit(6),
        name="arrange",
    )(inverse, arrived)


def teacher_kernel(features_ref, *refs):
    joined, weights, before, out_ref = refs[:2], refs[2:4], refs[4:-1], refs[-1]
    total = before[0][...] if before else None
    for joined_ref, weights_ref in zip(joined, weights):
        hidden = weights_ref.shape[1]
        held = jnp.maximum(dot(features_ref[...], weights_ref[...]), 0.0).astype(jnp.bfloat16)
        term = dot(held, joined_ref[:hidden, :]) + dot(held, joined_ref[hidden:, :])
        total = term if total is None else total + term
    out_ref[...] = total


def teacher(features, weights, joined, *before):
    return pl.pallas_call(
        teacher_kernel,
        out_shape=jax.ShapeDtypeStruct((features.shape[0], joined[0].shape[1]), jnp.float32),
        in_specs=[vmem] * (5 + len(before)),
        out_specs=vmem,
        compiler_params=limit(10),
        cost_estimate=pl.CostEstimate(flops=0, bytes_accessed=0, transcendentals=0),
        name="teacher",
    )(features, *joined, *weights, *before)


def student_kernel(
    scale, out_ref, here_ref, there_ref, pre_ref, hidden_ref, weights_ref, loss_ref, grad_ref, second_ref
):
    width = out_ref.shape[1]
    difference = out_ref[...] - (here_ref[...] + there_ref[...])
    out_grad = (scale * difference).astype(jnp.bfloat16)
    back = lax.dot_general(
        out_grad, weights_ref[...], (((1,), (1,)), ((), ())), preferred_element_type=jnp.float32
    )
    grad_ref[...] = jnp.where(pre_ref[...] > 0, back, 0.0).astype(jnp.bfloat16)
    second_ref[...] = lax.dot_general(
        hidden_ref[...], out_grad, (((0,), (0,)), ((), ())), preferred_element_type=jnp.float32
    ).astype(jnp.bfloat16)
    square = difference * difference
    total = square[:, :128]
    for column in range(128, width, 128):
        total = total + square[:, column : column + 128]
    loss_ref[...] = (0.5 / width) * jnp.sum(total.T, axis=0, keepdims=True)


def student(scale, student_out, here, there, student_pre, student_hidden, student_w2):
    samples, width = student_out.shape
    inner = student_pre.shape[1]
    return pl.pallas_call(
        lambda *refs: student_kernel(scale, *refs),
        out_shape=(
            jax.ShapeDtypeStruct((1, samples), jnp.float32),
            jax.ShapeDtypeStruct((samples, inner), jnp.bfloat16),
            jax.ShapeDtypeStruct((inner, width), jnp.bfloat16),
        ),
        in_specs=[vmem] * 6,
        out_specs=(vmem,) * 3,
        compiler_params=limit(8),
        name="student",
    )(student_out, here, there, student_pre, student_hidden, student_w2)


def turn_kernel(spot_ref, *refs):
    pieces, turned_ref = refs[:-1], refs[-1]
    span = pieces[0].shape[1] // 2
    start = spot_ref[0] * span
    high = spot_ref[1]
    for column in range(span // 128):
        columns = pl.ds(pl.multiple_of(start + column * 128, 128), 128)
        rows = jnp.concatenate([ref[:, columns] for ref in pieces], axis=0)
        for block in range(rows.shape[0] // 128):
            samples = slice(block * 128, (block + 1) * 128)
            turned = rows[samples].astype(jnp.float32).T
            for index in range(2):
                base = index * 64
                kept = jnp.where(
                    high == 0, turned[base : base + 32], turned[base + 32 : base + 64]
                ).astype(jnp.bfloat16)
                place = (2 * column + index) * 16
                for core in range(2):
                    turned_ref[core, place : place + 16, samples] = kept[core * 16 : core * 16 + 16]


def turn(spot, *pieces):
    samples = sum(piece.shape[0] for piece in pieces)
    return pl.pallas_call(
        turn_kernel,
        out_shape=jax.ShapeDtypeStruct((2, pieces[0].shape[1] // 8, samples), jnp.bfloat16),
        in_specs=[smem] + [vmem] * len(pieces),
        out_specs=vmem,
        compiler_params=limit(8),
        name="turn",
    )(spot, *pieces)


def gradient_kernel(spot_ref, early_ref, late_ref, *refs):
    grads, (mine_ref, other_ref) = refs[:4], refs[4:]
    core = spot_ref[2]
    grad = jnp.concatenate([ref[...] for ref in grads], axis=0)
    early = early_ref.shape[2]
    for ref, place in ((other_ref, 1 - core), (mine_ref, core)):
        total = dot(early_ref[place], grad[:early]) + dot(late_ref[place], grad[early:])
        ref[...] = total.astype(ref.dtype)


def gradients(spot, early, late, grads):
    shape = (early.shape[1], grads[0].shape[1])
    return pl.pallas_call(
        gradient_kernel,
        out_shape=(
            jax.ShapeDtypeStruct(shape, jnp.float32),
            jax.ShapeDtypeStruct(shape, jnp.bfloat16),
        ),
        in_specs=[smem] + [vmem] * 6,
        out_specs=(vmem, vmem),
        compiler_params=limit(8),
        name="gradients",
    )(spot, early, late, *grads)


def shards(
    pooled,
    counts,
    sample_order,
    table_order,
    teacher_w1,
    teacher_w2,
    projection,
    student_w1,
    student_w2,
):
    group = lax.axis_index("grp")
    member = lax.axis_index("mp")
    spot = jnp.stack([group, member // 2, member % 2]).astype(jnp.int32)
    tables = table_order.shape[0]
    block, width = pooled.shape[2:]
    samples = block // tables
    inner, outer = student_w2.shape

    near_w1 = swap(teacher_w1, NEAR)
    core_w1 = swap(teacher_w1, CORE)

    table_range = jnp.arange(tables, dtype=jnp.int32)
    inverse = jnp.sum(
        jnp.where(table_order[None, :] == table_range[:, None], table_range[None, :], 0), axis=1
    )
    divisor = jnp.maximum(counts[0, 0], 1).astype(jnp.float32)
    averaged = pooled[0, 0].astype(jnp.float32) / divisor[:, None]
    ordered = take_rows(averaged, sample_order)
    arrived = lax.all_to_all(
        ordered.reshape(tables, samples, width), "dp", split_axis=0, concat_axis=0, tiled=True
    )

    late_w2, _ = tie(teacher_w2, ordered)
    joined = split_two(dot(late_w2, projection))
    near_joined = swap(joined, NEAR)
    core_joined = swap(joined, CORE)
    near_w1, joined = tie(near_w1, joined)
    near_core_w1 = swap(near_w1, CORE)

    own = arrange(arrived, inverse)
    far = swap(own, FAR)
    near = swap(own, NEAR)

    student_pre = dot(own, student_w1)
    student_hidden = jax.nn.relu(student_pre).astype(jnp.bfloat16)
    student_out = dot(student_hidden, student_w2)
    chip = ((teacher_w1, core_w1), (joined, core_joined))
    here = teacher(own, *chip)

    far, near_joined, here, student_out = tie(far, near_joined, here, student_out)
    next_chip = ((near_w1, near_core_w1), (near_joined, swap(near_joined, CORE)))
    partial = teacher(far, *chip)
    partial = teacher(far, *next_chip, partial)
    there = swap(partial, FAR)
    opposite = swap(far, NEAR)
    later_own, _ = tie(own, partial)
    here = teacher(later_own, *next_chip, here)
    there, here, near = tie(there, here, near)
    early = turn(spot, own, near, far)

    devices = lax.axis_size("grp") * lax.axis_size("dp") * lax.axis_size("mp")
    grad_scale = 8192.0 / (samples * devices * outer)
    sample_loss, grad, second = student(
        grad_scale, student_out, here, there, student_pre, student_hidden, student_w2
    )
    grads = [grad] + [swap(grad, mask) for mask in (NEAR, FAR, OPPOSITE)]
    late = turn(spot, opposite)

    second = across(second)
    mine, other = gradients(spot, early, late, grads)
    first = (mine + swap(other, CORE).astype(jnp.float32)).astype(jnp.bfloat16)
    first, second = tie(first, second)
    grad_w1 = total_of(across(first), tables)
    second = total_of(second, tables)
    for mask in (NEAR, OPPOSITE, CORE):
        second = second + swap(second, mask)
    second = jnp.broadcast_to(second.astype(jnp.bfloat16)[None], (tables,) + second.shape)
    grad_w2 = across(second.reshape(inner, outer)).astype(jnp.float32)
    return (grad_w1, grad_w2, sample_loss)


def solution(mesh):
    return jax.shard_map(
        shards,
        mesh=mesh,
        in_specs=(
            P("dp", LINE, None, None),
            P("dp", LINE, None),
            P(LINE, None),
            P(),
            P(None, LINE),
            P(LINE, None),
            P(),
            P(),
            P(),
        ),
        out_specs=(P(("grp", "dp", "mp"), None), P(), P(LINE, "dp")),
        check_vma=False,
    )
```

time: 196 us -> 179 us (0.913)
  blocking collectives: 21.5 us -> 0 us
  starting transfers between devices: 42.8 us -> 52.8 us
  local copies, waits for them, and re-layouts: 12.1 us -> 5.12 us
  Pallas kernels: 22.3 us -> 24.9 us
  waiting for transfers between devices: 84.1 us -> 81.8 us
  matrix products: 2.87 us -> 5.06 us
    all_to_all x1 -> x0, blocking collectives: 21.5 us -> none  [shards(): lax.all_to_all(mine[:slab].reshape(tables, slab // tables, outer), 'dp',...]
    all_to_all x2 -> x3, starting transfers between devices: 9.47 us -> 25.8 us  [across(): return lax.all_to_all(values, 'dp', split_axis=0, concat_axis=0, tiled=True)]
    ppermute x21 -> x17, waiting for transfers between devices: 70.6 us -> 57 us  [swap(): lax.ppermute(values, LINE, [(index, index ^ mask) for index in range(8)])]
    all_to_all x2 -> x3, waiting for transfers between devices: 13.4 us -> 23.5 us  [across(): return lax.all_to_all(values, 'dp', split_axis=0, concat_axis=0, tiled=True)]
    ppermute x21 -> x17, starting transfers between devices: 22 us -> 15.7 us  [swap(): lax.ppermute(values, LINE, [(index, index ^ mask) for index in range(8)])]
    unnamed x44 -> x22, local copies, waits for them, and re-layouts: 9.64 us -> 4.27 us
    dot_general x3, matrix products: 2.87 us -> 5.06 us  [dot(): return jnp.dot(left, right, preferred_element_type=jnp.float32)]
    convert_element_type x0 -> x3, other arithmetic: none -> 2.1 us  [the longest x1 1.14 us: shards(): grad_w2 = across(second.reshape(inner, outer)).astype(jnp.float32)]
  transfers between devices with their start and end apart: 24 -> 21, of which waited for: 12 -> 15; matrix products, arithmetic and copies ran while one was open for 6% -> 6% of each run, Pallas kernels for 10% -> 14%
where the time goes in v2:
time: 179 us; the launch traced here: 178 us
  waiting for transfers between devices  81.8 us (46%)
  starting transfers between devices  52.8 us (29%)
  Pallas kernels  24.9 us (14%)
  other arithmetic  7.54 us (4%)
  local copies, waits for them, and re-layouts  5.12 us (3%)
  matrix products  5.06 us (3%)
    ppermute x17, waiting for transfers between devices, swap(): lax.ppermute(values, LINE, [(index, index ^ mask) for index in range(8)])  57 us
    all_to_all x3, starting transfers between devices, across(): return lax.all_to_all(values, 'dp', split_axis=0, concat_axis=0, tiled=True)  25.8 us
    all_to_all x3, waiting for transfers between devices, across(): return lax.all_to_all(values, 'dp', split_axis=0, concat_axis=0, tiled=True)  23.5 us
    ppermute x17, starting transfers between devices, swap(): lax.ppermute(values, LINE, [(index, index ^ mask) for index in range(8)])  15.7 us
    pallas_call x4, Pallas kernels, teacher(): pl.pallas_call(teacher_kernel, out_shape=jax.ShapeDtypeStruct((features.s...  12.2 us
    all_to_all x1, starting transfers between devices, shards(): lax.all_to_all(ordered.reshape(tables, samples, width), 'dp', split_axis=...  11.4 us
    pallas_call x1, Pallas kernels, take_rows(): pl.pallas_call(order_kernel, out_shape=jax.ShapeDtypeStruct(averaged.shap...  5.48 us
    dot_general x3, matrix products, dot(): return jnp.dot(left, right, preferred_element_type=jnp.float32)  5.06 us
  transfers between devices with their start and end apart: 21, of which 15 were waited for; matrix products, arithmetic and copies ran while one was open for 6% of the time, Pallas kernels for 14%

profile of v2, /device:TPU:32, one launch (start us, length us, event | category | flops | bytes accessed | tf_op | source)
XLA Modules:
  0.0 178.1 jit_solution(2436919832292206043)
XLA Ops:
  4.8 5.5 %take_rows.1 = bf16[4096,128]{1,0:T(8,128)(2,1)} custom-call(s32[1,4096]{1,0:T(1,128)S(1)} %copy-done.9, f32[4096,128]{1,0:T(8,128)S(1)} %convert_divide_fusion.averaged_ref), custom_call_target="tpu_custom_call" | custom-call | tf_op jit(solution)/shard_map/take_rows/pallas_call | solution.py:57
  10.2 11.4 %all-to-all-start = ((bf16[32,128,128]{2,1,0:T(8,128)(2,1)}), bf16[32,128,128]{2,1,0:T(8,128)(2,1)S(1)}, u32[]{:S(2)}, u32[]{:S(2)}) async-start(bf16[32,128,128]{2,1,0:T(8,128)(2,1)} %bitcast.5), calls=%async_computation | async-start | bytes 2097152 | tf_op jit(solution)/shard_map/all_to_all | solution.py:243
  21.7 1.9 %fusion = (bf16[256,512]{1,0:T(8,128)(2,1)S(1)}, f32[256,512]{1,0:T(8,128)S(1)}) fusion(bf16[256,2048]{1,0:T(8,128)(2,1)} %param.14, bf16[2048,512]{1,0:T(8,128)(2,1)S(1)} %copy-done), kind=kOutput, calls=%fused_computation.13 | convolution fusion | flops 537001984 | bytes 3932160 | tf_op jit(solution)/shard_map/dot_general | solution.py:25
  24.6 23.8 %collective-permute-done.2.refs_2_ = bf16[4096,256]{1,0:T(8,128)(2,1)} collective-permute-done((bf16[4096,256]{1,0:T(8,128)(2,1)}, bf16[4096,256]{1,0:T(8,128)(2,1)}, u32[]{:S(2)}, u32[]{:S(2)}) %collective-permute-start.2) | collective-permute-done | bytes 2097184 | tf_op jit(solution)/shard_map/ppermute | solution.py:29
  53.3 2.2 %collective-permute-start = (bf16[128,4096]{1,0:T(8,128)(2,1)S(1)}, bf16[128,4096]{1,0:T(8,128)(2,1)}, u32[]{:S(2)}, u32[]{:S(2)}) collective-permute-start(bf16[128,4096]{1,0:T(8,128)(2,1)S(1)} %arrange.1.features_ref.refs_0_), channel_id=1, source_target_pairs={{0,130},{1,131},{2,128},{3,129},{128,2},{129,3},{130,0},{131,1},{4... | collective-permute-start | bytes 3145736 | tf_op jit(solution)/shard_map/ppermute | solution.py:29
  56.0 2.9 %maximum_convert_fusion = (bf16[128,512]{1,0:T(8,128)(2,1)S(1)}, f32[128,512]{1,0:T(8,128)S(1)}) fusion(bf16[128,4096]{1,0:T(8,128)(2,1)S(1)} %arrange.1.features_ref.refs_0_, bf16[4096,512]{1,0:T(8,128)(2,1)} %param.16), kind=kOutput, calls=%fused_computation.7 | convolution fusion | flops 537001984 | bytes 5636096 | tf_op jit(solution)/shard_map/dot_general | solution.py:25
  60.7 2.6 %teacher.4.refs_4_ = f32[128,512]{1,0:T(8,128)S(1)} custom-call(bf16[128,4096]{1,0:T(8,128)(2,1)S(1)} %arrange.1.features_ref.refs_0_, bf16[512,512]{1,0:T(8,128)(2,1)S(1)} %copy-done.2, bf16[512,512]{1,0:T(8,128)(2,1)S(1)} %collective-permute-done.3.refs_1_, bf16[4096,256]{1,0:T(8,128)(2,1)S(1)} %copy-done.1, bf16[4096,256]{1,0:T(8,128)(2,1)} %collective-permute-done.4.refs_3_), custom_call_target="tpu_custom_call" | custom-call | tf_op jit(solution)/shard_map/teacher/pallas_call | solution.py:108
  63.3 6.8 %collective-permute-done.1.refs_0_ = bf16[512,512]{1,0:T(8,128)(2,1)S(1)} collective-permute-done((bf16[512,512]{1,0:T(8,128)(2,1)S(1)}, bf16[512,512]{1,0:T(8,128)(2,1)S(1)}, u32[]{:S(2)}, u32[]{:S(2)}) %collective-permute-start.1) | collective-permute-done | bytes 524320 | tf_op jit(solution)/shard_map/ppermute | solution.py:29
  70.2 8.8 %collective-permute-done.features_ref.refs_2_ = bf16[128,4096]{1,0:T(8,128)(2,1)} collective-permute-done((bf16[128,4096]{1,0:T(8,128)(2,1)S(1)}, bf16[128,4096]{1,0:T(8,128)(2,1)}, u32[]{:S(2)}, u32[]{:S(2)}) %collective-permute-start) | collective-permute-done | bytes 1048608 | tf_op jit(solution)/shard_map/ppermute | solution.py:29
  79.2 2.9 %teacher.5.refs_4_ = f32[128,512]{1,0:T(8,128)S(1)} custom-call(bf16[128,4096]{1,0:T(8,128)(2,1)} %collective-permute-done.features_ref.refs_2_, bf16[512,512]{1,0:T(8,128)(2,1)S(1)} %copy-done.2, bf16[512,512]{1,0:T(8,128)(2,1)S(1)} %collective-permute-done.3.refs_1_, bf16[4096,256]{1,0:T(8,128)(2,1)S(1)} %copy-done.1, ...), custom_call_target="tpu_custom_call" | custom-call | tf_op jit(solution)/shard_map/teacher/pallas_call | solution.py:108
  82.2 3.5 %teacher.6 = f32[128,512]{1,0:T(8,128)S(1)} custom-call(bf16[128,4096]{1,0:T(8,128)(2,1)} %collective-permute-done.features_ref.refs_2_, bf16[512,512]{1,0:T(8,128)(2,1)S(1)} %collective-permute-done.1.refs_0_, bf16[512,512]{1,0:T(8,128)(2,1)S(1)} %collective-permute-done.5.refs_1_, bf16[4096,256]{1,0:T(8,128)(2,1)} %collective-permute-done.2.refs_2_, ...), custom_call_target="tpu_custom_call" | custom-call | tf_op jit(solution)/shard_map/teacher/pallas_call | solution.py:108
  85.7 2.6 %collective-permute-start.7 = (f32[128,512]{1,0:T(8,128)S(1)}, f32[128,512]{1,0:T(8,128)S(1)}, u32[]{:S(2)}, u32[]{:S(2)}) collective-permute-start(f32[128,512]{1,0:T(8,128)S(1)} %teacher.6), channel_id=1, source_target_pairs={{0,130},{1,131},{2,128},{3,129},{128,2},{129,3},{130,0},{131,1},{4... | collective-permute-start | bytes 786440 | tf_op jit(solution)/shard_map/ppermute | solution.py:29
  88.3 3.2 %teacher.7.refs_1_ = f32[128,512]{1,0:T(8,128)S(1)} custom-call(bf16[128,4096]{1,0:T(8,128)(2,1)S(1)} %arrange.1.features_ref.refs_0_, bf16[512,512]{1,0:T(8,128)(2,1)S(1)} %collective-permute-done.1.refs_0_, bf16[512,512]{1,0:T(8,128)(2,1)S(1)} %collective-permute-done.5.refs_1_, bf16[4096,256]{1,0:T(8,128)(2,1)} %collective-permute-done.2.refs_2_, ...), custom_call_target="tpu_custom_call" | custom-call | tf_op jit(solution)/shard_map/teacher/pallas_call | solution.py:108
  92.6 3.1 %collective-permute-done.7.refs_2_ = f32[128,512]{1,0:T(8,128)S(1)} collective-permute-done((f32[128,512]{1,0:T(8,128)S(1)}, f32[128,512]{1,0:T(8,128)S(1)}, u32[]{:S(2)}, u32[]{:S(2)}) %collective-permute-start.7) | collective-permute-done | bytes 262176 | tf_op jit(solution)/shard_map/ppermute | solution.py:29
  97.4 11.4 %all-to-all-start.1 = ((bf16[32,16,512]{2,1,0:T(8,128)(2,1)}), bf16[32,16,512]{2,1,0:T(8,128)(2,1)}, u32[]{:S(2)}, u32[]{:S(2)}) async-start(bf16[32,16,512]{2,1,0:T(8,128)(2,1)} %bitcast.22), calls=%async_computation.1 | async-start | bytes 1048576 | tf_op jit(solution)/shard_map/all_to_all | solution.py:39
  109.9 2.4 %collective-permute-start.11 = (bf16[128,512]{1,0:T(8,128)(2,1)S(1)}, bf16[128,512]{1,0:T(8,128)(2,1)S(1)}, u32[]{:S(2)}, u32[]{:S(2)}) collective-permute-start(bf16[128,512]{1,0:T(8,128)(2,1)S(1)} %get-tuple-element.32.refs_0_), channel_id=1, source_target_pairs={{0,130},{1,131},{2,128},{3,129},{128,2},{129,3},{130,0},{131,1},{4... | collective-permute-start | bytes 393224 | tf_op jit(solution)/shard_map/ppermute | solution.py:29
  113.1 2.1 %collective-permute-done.9.refs_0_ = bf16[128,4096]{1,0:T(8,128)(2,1)} collective-permute-done((bf16[128,4096]{1,0:T(8,128)(2,1)}, bf16[128,4096]{1,0:T(8,128)(2,1)}, u32[]{:S(2)}, u32[]{:S(2)}) %collective-permute-start.9) | collective-permute-done | bytes 1048608 | tf_op jit(solution)/shard_map/ppermute | solution.py:29
  126.4 9.5 %all-to-all-start.2 = ((bf16[32,16,512]{2,1,0:T(8,128)(2,1)}), bf16[32,16,512]{2,1,0:T(8,128)(2,1)S(1)}, u32[]{:S(2)}, u32[]{:S(2)}) async-start(bf16[32,16,512]{2,1,0:T(8,128)(2,1)} %bitcast.8), calls=%async_computation.2 | async-start | bytes 1048576 | tf_op jit(solution)/shard_map/all_to_all | solution.py:39
  137.4 3.6 %collective-permute-done.14 = f32[16,512]{1,0:T(8,128)S(1)} collective-permute-done((f32[16,512]{1,0:T(8,128)S(1)}, f32[16,512]{1,0:T(8,128)S(1)}, u32[]{:S(2)}, u32[]{:S(2)}) %collective-permute-start.14) | collective-permute-done | bytes 32800 | tf_op jit(solution)/shard_map/ppermute | solution.py:29
  141.1 2.2 %collective-permute-start.15 = (f32[16,512]{1,0:T(8,128)S(1)}, f32[16,512]{1,0:T(8,128)S(1)}, u32[]{:S(2)}, u32[]{:S(2)}) collective-permute-start(f32[16,512]{1,0:T(8,128)S(1)} %add.19), channel_id=1, source_target_pairs={{0,2},{1,3},{2,0},{3,1},{128,130},{129,131},{130,128},{131,129},{4... | collective-permute-start | bytes 98312 | tf_op jit(solution)/shard_map/ppermute | solution.py:29
  143.3 3.2 %collective-permute-done.15 = f32[16,512]{1,0:T(8,128)S(1)} collective-permute-done((f32[16,512]{1,0:T(8,128)S(1)}, f32[16,512]{1,0:T(8,128)S(1)}, u32[]{:S(2)}, u32[]{:S(2)}) %collective-permute-start.15) | collective-permute-done | bytes 32800 | tf_op jit(solution)/shard_map/ppermute | solution.py:29
  147.7 6.2 %all-to-all-done.2 = bf16[32,16,512]{2,1,0:T(8,128)(2,1)S(1)} async-done(((bf16[32,16,512]{2,1,0:T(8,128)(2,1)}), bf16[32,16,512]{2,1,0:T(8,128)(2,1)S(1)}, u32[]{:S(2)}, u32[]{:S(2)}) %all-to-all-start.2) | async-done | bytes 524320 | tf_op jit(solution)/shard_map/all_to_all | solution.py:39
  154.7 4.8 %all-to-all-start.3 = ((bf16[32,16,512]{2,1,0:T(8,128)(2,1)}), bf16[32,16,512]{2,1,0:T(8,128)(2,1)S(1)}, u32[]{:S(2)}, u32[]{:S(2)}) async-start(bf16[32,16,512]{2,1,0:T(8,128)(2,1)} %broadcast_in_dim.24), calls=%async_computation.3 | async-start | bytes 1048576 | tf_op jit(solution)/shard_map/all_to_all | solution.py:39
  160.3 16.7 %all-to-all-done.3 = bf16[32,16,512]{2,1,0:T(8,128)(2,1)S(1)} async-done(((bf16[32,16,512]{2,1,0:T(8,128)(2,1)}), bf16[32,16,512]{2,1,0:T(8,128)(2,1)S(1)}, u32[]{:S(2)}, u32[]{:S(2)}) %all-to-all-start.3) | async-done | bytes 524320 | tf_op jit(solution)/shard_map/all_to_all | solution.py:39
  (67 shorter events, 33.9 us)
Async XLA Ops:
  0.6 21.1 %copy-start = (bf16[2048,512]{1,0:T(8,128)(2,1)S(1)}, bf16[2048,512]{1,0:T(8,128)(2,1)}, u32[]{:S(2)}) copy-start(bf16[2048,512]{1,0:T(8,128)(2,1)} %param.15) | copy-start | bytes 6291460
  0.7 47.8 %collective-permute-start.2 = (bf16[4096,256]{1,0:T(8,128)(2,1)}, bf16[4096,256]{1,0:T(8,128)(2,1)}, u32[]{:S(2)}, u32[]{:S(2)}) collective-permute-start(bf16[4096,256]{1,0:T(8,128)(2,1)} %refs_2_.3), channel_id=1, source_target_pairs={{0,128},{1,129},{2,130},{3,131},{128,0},{129,1},{130,2},{131,3},{4... | collective-permute-start | bytes 6291464 | tf_op jit(solution)/shard_map/ppermute | solution.py:29
  10.2 39.6 %all-to-all-start = ((bf16[32,128,128]{2,1,0:T(8,128)(2,1)}), bf16[32,128,128]{2,1,0:T(8,128)(2,1)S(1)}, u32[]{:S(2)}, u32[]{:S(2)}) async-start(bf16[32,128,128]{2,1,0:T(8,128)(2,1)} %bitcast.5), calls=%async_computation | async-start | bytes 2097152 | tf_op jit(solution)/shard_map/all_to_all | solution.py:243
  21.6 26.8 %copy-start.10 = (s32[32]{0:T(128)S(1)}, s32[32]{0:T(128)}, u32[]{:S(2)}) copy-start(s32[32]{0:T(128)} %param.12) | copy-start | bytes 388
  21.6 39.1 %collective-permute-start.4 = (bf16[4096,256]{1,0:T(8,128)(2,1)}, bf16[4096,256]{1,0:T(8,128)(2,1)}, u32[]{:S(2)}, u32[]{:S(2)}) collective-permute-start(bf16[4096,256]{1,0:T(8,128)(2,1)} %refs_2_.3), channel_id=1, source_target_pairs={{0,1},{1,0},{2,3},{3,2},{128,129},{129,128},{130,131},{131,130},{4... | collective-permute-start | bytes 6291464 | tf_op jit(solution)/shard_map/ppermute | solution.py:29
  48.4 33.7 %collective-permute-start.6 = (bf16[4096,256]{1,0:T(8,128)(2,1)}, bf16[4096,256]{1,0:T(8,128)(2,1)}, u32[]{:S(2)}, u32[]{:S(2)}) collective-permute-start(bf16[4096,256]{1,0:T(8,128)(2,1)} %collective-permute-done.2.refs_2_), channel_id=1, source_target_pairs={{0,1},{1,0},{2,3},{3,2},{128,129},{129,128},{130,131},{131,130},{4... | collective-permute-start | bytes 6291464 | tf_op jit(solution)/shard_map/ppermute | solution.py:29
  53.2 7.5 %copy-start.1 = (bf16[4096,256]{1,0:T(8,128)(2,1)S(1)}, bf16[4096,256]{1,0:T(8,128)(2,1)}, u32[]{:S(2)}) copy-start(bf16[4096,256]{1,0:T(8,128)(2,1)} %refs_2_.3) | copy-start | bytes 6291460
  53.3 25.7 %collective-permute-start = (bf16[128,4096]{1,0:T(8,128)(2,1)S(1)}, bf16[128,4096]{1,0:T(8,128)(2,1)}, u32[]{:S(2)}, u32[]{:S(2)}) collective-permute-start(bf16[128,4096]{1,0:T(8,128)(2,1)S(1)} %arrange.1.features_ref.refs_0_), channel_id=1, source_target_pairs={{0,130},{1,131},{2,128},{3,129},{128,2},{129,3},{130,0},{131,1},{4... | collective-permute-start | bytes 3145736 | tf_op jit(solution)/shard_map/ppermute | solution.py:29
  55.4 3.5 %collective-permute-start.3 = (bf16[512,512]{1,0:T(8,128)(2,1)S(1)}, bf16[512,512]{1,0:T(8,128)(2,1)S(1)}, u32[]{:S(2)}, u32[]{:S(2)}) collective-permute-start(bf16[512,512]{1,0:T(8,128)(2,1)S(1)} %copy-done.2), channel_id=1, source_target_pairs={{0,1},{1,0},{2,3},{3,2},{128,129},{129,128},{130,131},{131,130},{4... | collective-permute-start | bytes 1572872 | tf_op jit(solution)/shard_map/ppermute | solution.py:29
  55.4 14.7 %collective-permute-start.1 = (bf16[512,512]{1,0:T(8,128)(2,1)S(1)}, bf16[512,512]{1,0:T(8,128)(2,1)S(1)}, u32[]{:S(2)}, u32[]{:S(2)}) collective-permute-start(bf16[512,512]{1,0:T(8,128)(2,1)S(1)} %copy-done.2), channel_id=1, source_target_pairs={{0,128},{1,129},{2,130},{3,131},{128,0},{129,1},{130,2},{131,3},{4... | collective-permute-start | bytes 1572872 | tf_op jit(solution)/shard_map/ppermute | solution.py:29
  59.0 33.7 %collective-permute-start.8 = (bf16[128,4096]{1,0:T(8,128)(2,1)S(1)}, bf16[128,4096]{1,0:T(8,128)(2,1)S(1)}, u32[]{:S(2)}, u32[]{:S(2)}) collective-permute-start(bf16[128,4096]{1,0:T(8,128)(2,1)S(1)} %arrange.1.features_ref.refs_0_), channel_id=1, source_target_pairs={{0,128},{1,129},{2,130},{3,131},{128,0},{129,1},{130,2},{131,3},{4... | collective-permute-start | bytes 3145736 | tf_op jit(solution)/shard_map/ppermute | solution.py:29
  78.9 36.3 %collective-permute-start.9 = (bf16[128,4096]{1,0:T(8,128)(2,1)}, bf16[128,4096]{1,0:T(8,128)(2,1)}, u32[]{:S(2)}, u32[]{:S(2)}) collective-permute-start(bf16[128,4096]{1,0:T(8,128)(2,1)} %collective-permute-done.features_ref.refs_2_), channel_id=1, source_target_pairs={{0,128},{1,129},{2,130},{3,131},{128,0},{129,1},{130,2},{131,3},{4... | collective-permute-start | bytes 3145736 | tf_op jit(solution)/shard_map/ppermute | solution.py:29
  79.2 2.9 %collective-permute-start.5 = (bf16[512,512]{1,0:T(8,128)(2,1)S(1)}, bf16[512,512]{1,0:T(8,128)(2,1)S(1)}, u32[]{:S(2)}, u32[]{:S(2)}) collective-permute-start(bf16[512,512]{1,0:T(8,128)(2,1)S(1)} %collective-permute-done.1.refs_0_), channel_id=1, source_target_pairs={{0,1},{1,0},{2,3},{3,2},{128,129},{129,128},{130,131},{131,130},{4... | collective-permute-start | bytes 1572872 | tf_op jit(solution)/shard_map/ppermute | solution.py:29
  85.7 10.0 %collective-permute-start.7 = (f32[128,512]{1,0:T(8,128)S(1)}, f32[128,512]{1,0:T(8,128)S(1)}, u32[]{:S(2)}, u32[]{:S(2)}) collective-permute-start(f32[128,512]{1,0:T(8,128)S(1)} %teacher.6), channel_id=1, source_target_pairs={{0,130},{1,131},{2,128},{3,129},{128,2},{129,3},{130,0},{131,1},{4... | collective-permute-start | bytes 786440 | tf_op jit(solution)/shard_map/ppermute | solution.py:29
  97.4 29.0 %all-to-all-start.1 = ((bf16[32,16,512]{2,1,0:T(8,128)(2,1)}), bf16[32,16,512]{2,1,0:T(8,128)(2,1)}, u32[]{:S(2)}, u32[]{:S(2)}) async-start(bf16[32,16,512]{2,1,0:T(8,128)(2,1)} %bitcast.22), calls=%async_computation.1 | async-start | bytes 1048576 | tf_op jit(solution)/shard_map/all_to_all | solution.py:39
  108.9 10.8 %collective-permute-start.10 = (bf16[128,512]{1,0:T(8,128)(2,1)S(1)}, bf16[128,512]{1,0:T(8,128)(2,1)S(1)}, u32[]{:S(2)}, u32[]{:S(2)}) collective-permute-start(bf16[128,512]{1,0:T(8,128)(2,1)S(1)} %get-tuple-element.32.refs_0_), channel_id=1, source_target_pairs={{0,128},{1,129},{2,130},{3,131},{128,0},{129,1},{130,2},{131,3},{4... | collective-permute-start | bytes 393224 | tf_op jit(solution)/shard_map/ppermute | solution.py:29
  109.9 9.8 %collective-permute-start.11 = (bf16[128,512]{1,0:T(8,128)(2,1)S(1)}, bf16[128,512]{1,0:T(8,128)(2,1)S(1)}, u32[]{:S(2)}, u32[]{:S(2)}) collective-permute-start(bf16[128,512]{1,0:T(8,128)(2,1)S(1)} %get-tuple-element.32.refs_0_), channel_id=1, source_target_pairs={{0,130},{1,131},{2,128},{3,129},{128,2},{129,3},{130,0},{131,1},{4... | collective-permute-start | bytes 393224 | tf_op jit(solution)/shard_map/ppermute | solution.py:29
  112.3 8.8 %collective-permute-start.12 = (bf16[128,512]{1,0:T(8,128)(2,1)S(1)}, bf16[128,512]{1,0:T(8,128)(2,1)}, u32[]{:S(2)}, u32[]{:S(2)}) collective-permute-start(bf16[128,512]{1,0:T(8,128)(2,1)S(1)} %get-tuple-element.32.refs_0_), channel_id=1, source_target_pairs={{0,2},{1,3},{2,0},{3,1},{128,130},{129,131},{130,128},{131,129},{4... | collective-permute-start | bytes 393224 | tf_op jit(solution)/shard_map/ppermute | solution.py:29
  122.9 2.0 %collective-permute-start.13 = (bf16[512,512]{1,0:T(8,128)(2,1)S(1)}, bf16[512,512]{1,0:T(8,128)(2,1)S(1)}, u32[]{:S(2)}, u32[]{:S(2)}) collective-permute-start(bf16[512,512]{1,0:T(8,128)(2,1)S(1)} %get-tuple-element.34), channel_id=1, source_target_pairs={{0,1},{1,0},{2,3},{3,2},{128,129},{129,128},{130,131},{131,130},{4... | collective-permute-start | bytes 1572872 | tf_op jit(solution)/shard_map/ppermute | solution.py:29
  126.4 27.4 %all-to-all-start.2 = ((bf16[32,16,512]{2,1,0:T(8,128)(2,1)}), bf16[32,16,512]{2,1,0:T(8,128)(2,1)S(1)}, u32[]{:S(2)}, u32[]{:S(2)}) async-start(bf16[32,16,512]{2,1,0:T(8,128)(2,1)} %bitcast.8), calls=%async_computation.2 | async-start | bytes 1048576 | tf_op jit(solution)/shard_map/all_to_all | solution.py:39
  137.1 4.0 %collective-permute-start.14 = (f32[16,512]{1,0:T(8,128)S(1)}, f32[16,512]{1,0:T(8,128)S(1)}, u32[]{:S(2)}, u32[]{:S(2)}) collective-permute-start(f32[16,512]{1,0:T(8,128)S(1)} %convert_reduce_fusion), channel_id=1, source_target_pairs={{0,128},{1,129},{2,130},{3,131},{128,0},{129,1},{130,2},{131,3},{4... | collective-permute-start | bytes 98312 | tf_op jit(solution)/shard_map/ppermute | solution.py:29
  141.1 5.4 %collective-permute-start.15 = (f32[16,512]{1,0:T(8,128)S(1)}, f32[16,512]{1,0:T(8,128)S(1)}, u32[]{:S(2)}, u32[]{:S(2)}) collective-permute-start(f32[16,512]{1,0:T(8,128)S(1)} %add.19), channel_id=1, source_target_pairs={{0,2},{1,3},{2,0},{3,1},{128,130},{129,131},{130,128},{131,129},{4... | collective-permute-start | bytes 98312 | tf_op jit(solution)/shard_map/ppermute | solution.py:29
  146.5 1.2 collective-permute-start.16
  154.7 22.3 %all-to-all-start.3 = ((bf16[32,16,512]{2,1,0:T(8,128)(2,1)}), bf16[32,16,512]{2,1,0:T(8,128)(2,1)S(1)}, u32[]{:S(2)}, u32[]{:S(2)}) async-start(bf16[32,16,512]{2,1,0:T(8,128)(2,1)} %broadcast_in_dim.24), calls=%async_computation.3 | async-start | bytes 1048576 | tf_op jit(solution)/shard_map/all_to_all | solution.py:39
  (8 other events, 23.0 us)

commit v3 on v2

--- a/solution.py
+++ b/solution.py
@@ -64,20 +64,10 @@
     )(order, averaged)
 
 
-def arrange_kernel(inverse_ref, arrived_ref, features_ref, semaphores):
+def arrange_kernel(inverse_ref, arrived_ref, features_ref):
     tables, _, width = arrived_ref.shape
-    copies = [
-        pltpu.make_async_copy(
-            arrived_ref.at[inverse_ref[column]],
-            features_ref.at[:, column * width : (column + 1) * width],
-            semaphores.at[column],
-        )
-        for column in range(tables)
-    ]
-    for copy in copies:
-        copy.start()
-    for copy in copies:
-        copy.wait()
+    for column in range(tables):
+        features_ref[:, column * width : (column + 1) * width] = arrived_ref[inverse_ref[column]]
 
 
 def arrange(arrived, inverse):
@@ -85,9 +75,8 @@
     return pl.pallas_call(
         arrange_kernel,
         out_shape=jax.ShapeDtypeStruct((rows, tables * width), arrived.dtype),
-        in_specs=[smem, pl.BlockSpec(memory_space=pltpu.HBM)],
+        in_specs=[smem, vmem],
         out_specs=vmem,
-        scratch_shapes=[pltpu.SemaphoreType.DMA((tables,))],
         compiler_params=limit(6),
         name="arrange",
     )(inverse, arrived)
@@ -101,13 +90,13 @@
         held = jnp.maximum(dot(features_ref[...], weights_ref[...]), 0.0).astype(jnp.bfloat16)
         term = dot(held, joined_ref[:hidden, :]) + dot(held, joined_ref[hidden:, :])
         total = term if total is None else total + term
-    out_ref[...] = total
-
-
-def teacher(features, weights, joined, *before):
+    out_ref[...] = total.astype(out_ref.dtype)
+
+
+def teacher(features, weights, joined, *before, kept=jnp.float32):
     return pl.pallas_call(
         teacher_kernel,
-        out_shape=jax.ShapeDtypeStruct((features.shape[0], joined[0].shape[1]), jnp.float32),
+        out_shape=jax.ShapeDtypeStruct((features.shape[0], joined[0].shape[1]), kept),
         in_specs=[vmem] * (5 + len(before)),
         out_specs=vmem,
         compiler_params=limit(10),
@@ -120,7 +109,7 @@
     scale, out_ref, here_ref, there_ref, pre_ref, hidden_ref, weights_ref, loss_ref, grad_ref, second_ref
 ):
     width = out_ref.shape[1]
-    difference = out_ref[...] - (here_ref[...] + there_ref[...])
+    difference = out_ref[...] - (here_ref[...] + there_ref[...].astype(jnp.float32))
     out_grad = (scale * difference).astype(jnp.bfloat16)
     back = lax.dot_general(
         out_grad, weights_ref[...], (((1,), (1,)), ((), ())), preferred_element_type=jnp.float32
@@ -248,10 +237,10 @@
     joined = split_two(dot(late_w2, projection))
     near_joined = swap(joined, NEAR)
     core_joined = swap(joined, CORE)
-    near_w1, joined = tie(near_w1, joined)
+    arrived, near_w1, joined = tie(arrived, near_w1, joined)
+
+    own = arrange(arrived, inverse)
     near_core_w1 = swap(near_w1, CORE)
-
-    own = arrange(arrived, inverse)
     far = swap(own, FAR)
     near = swap(own, NEAR)
 
@@ -264,7 +253,7 @@
     far, near_joined, here, student_out = tie(far, near_joined, here, student_out)
     next_chip = ((near_w1, near_core_w1), (near_joined, swap(near_joined, CORE)))
     partial = teacher(far, *chip)
-    partial = teacher(far, *next_chip, partial)
+    partial = teacher(far, *next_chip, partial, kept=jnp.bfloat16)
     there = swap(partial, FAR)
     opposite = swap(far, NEAR)
     later_own, _ = tie(own, partial)
@@ -278,18 +267,28 @@
         grad_scale, student_out, here, there, student_pre, student_hidden, student_w2
     )
     grads = [grad] + [swap(grad, mask) for mask in (NEAR, FAR, OPPOSITE)]
+    opposite, early = tie(opposite, early)
     late = turn(spot, opposite)
 
     second = across(second)
     mine, other = gradients(spot, early, late, grads)
     first = (mine + swap(other, CORE).astype(jnp.float32)).astype(jnp.bfloat16)
     first, second = tie(first, second)
-    grad_w1 = total_of(across(first), tables)
+    first = across(first)
     second = total_of(second, tables)
     for mask in (NEAR, OPPOSITE, CORE):
         second = second + swap(second, mask)
-    second = jnp.broadcast_to(second.astype(jnp.bfloat16)[None], (tables,) + second.shape)
-    grad_w2 = across(second.reshape(inner, outer)).astype(jnp.float32)
+    second, first = tie(second, first)
+    grad_w1 = total_of(first, tables)
+    count = second.shape[0] // 2
+    second = lax.dynamic_slice_in_dim(second, spot[2] * count, count, axis=0).astype(jnp.bfloat16)
+    second = across(jnp.broadcast_to(second[None], (tables, count, outer)))
+    third = swap(second, CORE)
+    grad_w2 = jnp.where(
+        spot[2] == 0,
+        jnp.concatenate([second, third], axis=1),
+        jnp.concatenate([third, second], axis=1),
+    ).astype(jnp.float32).reshape(inner, outer)
     return (grad_w1, grad_w2, sample_loss)
 
 

time: 179 us -> 174 us (0.972)
  blocking collectives: 0 us -> 16.7 us
  waiting for transfers between devices: 81.8 us -> 70.2 us
  starting transfers between devices: 52.8 us -> 45.3 us
  matrix products: 5.06 us -> 2.93 us
    all_to_all x1, waiting for transfers between devices: 1.3 us -> 25.3 us  [shards(): lax.all_to_all(ordered.reshape(tables, samples, width), 'dp', split_axis=...]
    ppermute x17 -> x18, waiting for transfers between devices: 57 us -> 38.8 us  [swap(): lax.ppermute(values, LINE, [(index, index ^ mask) for index in range(8)])]
    all_to_all x3 -> x2, waiting for transfers between devices: 23.5 us -> 6.16 us  [across(): return lax.all_to_all(values, 'dp', split_axis=0, concat_axis=0, tiled=True)]
    all_to_all x0 -> x1, blocking collectives: none -> 16.7 us  [across(): return lax.all_to_all(values, 'dp', split_axis=0, concat_axis=0, tiled=True)]
    all_to_all x3 -> x2, starting transfers between devices: 25.8 us -> 18.5 us  [across(): return lax.all_to_all(values, 'dp', split_axis=0, concat_axis=0, tiled=True)]
    dot_general x3, matrix products: 5.06 us -> 2.93 us  [dot(): return jnp.dot(left, right, preferred_element_type=jnp.float32)]
    ppermute x17 -> x18, starting transfers between devices: 15.7 us -> 15.5 us  [swap(): lax.ppermute(values, LINE, [(index, index ^ mask) for index in range(8)])]
  transfers between devices with their start and end apart: 21 -> 21, of which waited for: 15 -> 14; matrix products, arithmetic and copies ran while one was open for 6% -> 5% of each run, Pallas kernels for 14% -> 14%
where the time goes in v3:
time: 174 us; the launch traced here: 172 us
  waiting for transfers between devices  70.2 us (40%)
  starting transfers between devices  45.3 us (26%)
  Pallas kernels  23.7 us (14%)
  blocking collectives  16.7 us (10%)
  other arithmetic  7.76 us (4%)
  local copies, waits for them, and re-layouts  4.53 us (3%)
  matrix products  2.93 us (2%)
    ppermute x18, waiting for transfers between devices, swap(): lax.ppermute(values, LINE, [(index, index ^ mask) for index in range(8)])  38.8 us
    all_to_all x1, waiting for transfers between devices, shards(): lax.all_to_all(ordered.reshape(tables, samples, width), 'dp', split_axis=...  25.3 us
    all_to_all x2, starting transfers between devices, across(): return lax.all_to_all(values, 'dp', split_axis=0, concat_axis=0, tiled=True)  18.5 us
    all_to_all x1, blocking collectives, across(): return lax.all_to_all(values, 'dp', split_axis=0, concat_axis=0, tiled=True)  16.7 us
    ppermute x18, starting transfers between devices, swap(): lax.ppermute(values, LINE, [(index, index ^ mask) for index in range(8)])  15.5 us
    pallas_call x4, Pallas kernels, teacher(): pl.pallas_call(teacher_kernel, out_shape=jax.ShapeDtypeStruct((features.s...  11.4 us
    all_to_all x1, starting transfers between devices, shards(): lax.all_to_all(ordered.reshape(tables, samples, width), 'dp', split_axis=...  11.4 us
    all_to_all x2, waiting for transfers between devices, across(): return lax.all_to_all(values, 'dp', split_axis=0, concat_axis=0, tiled=True)  6.16 us
  transfers between devices with their start and end apart: 21, of which 14 were waited for; matrix products, arithmetic and copies ran while one was open for 5% of the time, Pallas kernels for 14%

profile of v3, /device:TPU:32, one launch (start us, length us, event | category | flops | bytes accessed | tf_op | source)
XLA Modules:
  0.0 172.1 jit_solution(2522237698632921632)
XLA Ops:
  4.8 5.5 %take_rows.1 = bf16[4096,128]{1,0:T(8,128)(2,1)} custom-call(s32[1,4096]{1,0:T(1,128)S(1)} %copy-done.8, f32[4096,128]{1,0:T(8,128)S(1)} %convert_divide_fusion.averaged_ref), custom_call_target="tpu_custom_call" | custom-call | tf_op jit(solution)/shard_map/take_rows/pallas_call | solution.py:57
  10.2 11.4 %all-to-all-start = ((bf16[32,128,128]{2,1,0:T(8,128)(2,1)}), bf16[32,128,128]{2,1,0:T(8,128)(2,1)S(1)}, u32[]{:S(2)}, u32[]{:S(2)}) async-start(bf16[32,128,128]{2,1,0:T(8,128)(2,1)} %bitcast.5), calls=%async_computation | async-start | bytes 2097152 | tf_op jit(solution)/shard_map/all_to_all | solution.py:232
  21.7 1.9 %fusion = (bf16[256,512]{1,0:T(8,128)(2,1)S(1)}, f32[256,512]{1,0:T(8,128)S(1)}) fusion(bf16[256,2048]{1,0:T(8,128)(2,1)} %param.14, bf16[2048,512]{1,0:T(8,128)(2,1)S(1)} %copy-done), kind=kOutput, calls=%fused_computation.14 | convolution fusion | flops 537001984 | bytes 3932160 | tf_op jit(solution)/shard_map/dot_general | solution.py:25
  24.6 25.3 %all-to-all-done.arrived_ref = bf16[32,128,128]{2,1,0:T(8,128)(2,1)S(1)} async-done(((bf16[32,128,128]{2,1,0:T(8,128)(2,1)}), bf16[32,128,128]{2,1,0:T(8,128)(2,1)S(1)}, u32[]{:S(2)}, u32[]{:S(2)}) %all-to-all-start) | async-done | bytes 1048608 | tf_op jit(solution)/shard_map/all_to_all | solution.py:232
  53.5 2.2 %collective-permute-start.1 = (bf16[128,4096]{1,0:T(8,128)(2,1)S(1)}, bf16[128,4096]{1,0:T(8,128)(2,1)}, u32[]{:S(2)}, u32[]{:S(2)}) collective-permute-start(bf16[128,4096]{1,0:T(8,128)(2,1)S(1)} %arrange.1.features_ref.refs_0_), channel_id=1, source_target_pairs={{0,130},{1,131},{2,128},{3,129},{128,2},{129,3},{130,0},{131,1},{4... | collective-permute-start | bytes 3145736 | tf_op jit(solution)/shard_map/ppermute | solution.py:29
  57.8 2.8 %teacher.4.refs_4_ = f32[128,512]{1,0:T(8,128)S(1)} custom-call(bf16[128,4096]{1,0:T(8,128)(2,1)S(1)} %arrange.1.features_ref.refs_0_, bf16[512,512]{1,0:T(8,128)(2,1)} %pad_maximum_fusion.refs_0_, bf16[512,512]{1,0:T(8,128)(2,1)S(1)} %collective-permute-done.3.refs_1_, bf16[4096,256]{1,0:T(8,128)(2,1)S(1)} %copy-done.1, ...), custom_call_target="tpu_custom_call" | custom-call | tf_op jit(solution)/shard_map/teacher/pallas_call | solution.py:97
  61.8 8.9 %collective-permute-done.2.refs_0_ = bf16[512,512]{1,0:T(8,128)(2,1)S(1)} collective-permute-done((bf16[512,512]{1,0:T(8,128)(2,1)}, bf16[512,512]{1,0:T(8,128)(2,1)S(1)}, u32[]{:S(2)}, u32[]{:S(2)}) %collective-permute-start.2) | collective-permute-done | bytes 524320 | tf_op jit(solution)/shard_map/ppermute | solution.py:29
  70.7 9.3 %collective-permute-done.1.features_ref.refs_2_ = bf16[128,4096]{1,0:T(8,128)(2,1)} collective-permute-done((bf16[128,4096]{1,0:T(8,128)(2,1)S(1)}, bf16[128,4096]{1,0:T(8,128)(2,1)}, u32[]{:S(2)}, u32[]{:S(2)}) %collective-permute-start.1) | collective-permute-done | bytes 1048608 | tf_op jit(solution)/shard_map/ppermute | solution.py:29
  80.1 3.1 %teacher.5.refs_4_ = f32[128,512]{1,0:T(8,128)S(1)} custom-call(bf16[128,4096]{1,0:T(8,128)(2,1)} %collective-permute-done.1.features_ref.refs_2_, bf16[512,512]{1,0:T(8,128)(2,1)} %pad_maximum_fusion.refs_0_, bf16[512,512]{1,0:T(8,128)(2,1)S(1)} %collective-permute-done.3.refs_1_, bf16[4096,256]{1,0:T(8,128)(2,1)S(1)} %copy-done.1, ...), custom_call_target="tpu_custom_call" | custom-call | tf_op jit(solution)/shard_map/teacher/pallas_call | solution.py:97
  83.2 2.9 %teacher.6 = bf16[128,512]{1,0:T(8,128)(2,1)S(1)} custom-call(bf16[128,4096]{1,0:T(8,128)(2,1)} %collective-permute-done.1.features_ref.refs_2_, bf16[512,512]{1,0:T(8,128)(2,1)S(1)} %collective-permute-done.2.refs_0_, bf16[512,512]{1,0:T(8,128)(2,1)S(1)} %collective-permute-done.6.refs_1_, bf16[4096,256]{1,0:T(8,128)(2,1)} %collective-permute-done.refs_2_, ...), custom_call_target="tpu_custom_call" | custom-call | tf_op jit(solution)/shard_map/teacher/pallas_call | solution.py:97
  86.1 2.2 %collective-permute-start.8 = (bf16[128,512]{1,0:T(8,128)(2,1)S(1)}, bf16[128,512]{1,0:T(8,128)(2,1)S(1)}, u32[]{:S(2)}, u32[]{:S(2)}) collective-permute-start(bf16[128,512]{1,0:T(8,128)(2,1)S(1)} %teacher.6), channel_id=1, source_target_pairs={{0,130},{1,131},{2,128},{3,129},{128,2},{129,3},{130,0},{131,1},{4... | collective-permute-start | bytes 393224 | tf_op jit(solution)/shard_map/ppermute | solution.py:29
  88.3 2.6 %teacher.7.refs_1_ = f32[128,512]{1,0:T(8,128)S(1)} custom-call(bf16[128,4096]{1,0:T(8,128)(2,1)S(1)} %arrange.1.features_ref.refs_0_, bf16[512,512]{1,0:T(8,128)(2,1)S(1)} %collective-permute-done.2.refs_0_, bf16[512,512]{1,0:T(8,128)(2,1)S(1)} %collective-permute-done.6.refs_1_, bf16[4096,256]{1,0:T(8,128)(2,1)} %collective-permute-done.refs_2_, ...), custom_call_target="tpu_custom_call" | custom-call | tf_op jit(solution)/shard_map/teacher/pallas_call | solution.py:97
  90.9 2.3 %collective-permute-done.9.refs_1_ = bf16[128,4096]{1,0:T(8,128)(2,1)S(1)} collective-permute-done((bf16[128,4096]{1,0:T(8,128)(2,1)S(1)}, bf16[128,4096]{1,0:T(8,128)(2,1)S(1)}, u32[]{:S(2)}, u32[]{:S(2)}) %collective-permute-start.9) | collective-permute-done | bytes 1048608 | tf_op jit(solution)/shard_map/ppermute | solution.py:29
  95.0 9.6 %all-to-all-start.1 = ((bf16[32,16,512]{2,1,0:T(8,128)(2,1)}), bf16[32,16,512]{2,1,0:T(8,128)(2,1)}, u32[]{:S(2)}, u32[]{:S(2)}) async-start(bf16[32,16,512]{2,1,0:T(8,128)(2,1)} %bitcast.25), calls=%async_computation.1 | async-start | bytes 1048576 | tf_op jit(solution)/shard_map/all_to_all | solution.py:39
  105.3 2.3 %collective-permute-start.11 = (bf16[128,512]{1,0:T(8,128)(2,1)S(1)}, bf16[128,512]{1,0:T(8,128)(2,1)S(1)}, u32[]{:S(2)}, u32[]{:S(2)}) collective-permute-start(bf16[128,512]{1,0:T(8,128)(2,1)S(1)} %get-tuple-element.40.refs_0_), channel_id=1, source_target_pairs={{0,130},{1,131},{2,128},{3,129},{128,2},{129,3},{130,0},{131,1},{4... | collective-permute-start | bytes 393224 | tf_op jit(solution)/shard_map/ppermute | solution.py:29
  112.0 3.8 %collective-permute-done.5.refs_0_ = bf16[128,4096]{1,0:T(8,128)(2,1)} collective-permute-done((bf16[128,4096]{1,0:T(8,128)(2,1)}, bf16[128,4096]{1,0:T(8,128)(2,1)}, u32[]{:S(2)}, u32[]{:S(2)}) %collective-permute-start.5) | collective-permute-done | bytes 1048608 | tf_op jit(solution)/shard_map/ppermute | solution.py:29
  118.5 2.3 %collective-permute-done.12.refs_3_ = bf16[128,512]{1,0:T(8,128)(2,1)} collective-permute-done((bf16[128,512]{1,0:T(8,128)(2,1)S(1)}, bf16[128,512]{1,0:T(8,128)(2,1)}, u32[]{:S(2)}, u32[]{:S(2)}) %collective-permute-start.12) | collective-permute-done | bytes 131104 | tf_op jit(solution)/shard_map/ppermute | solution.py:29
  122.8 1.9 %collective-permute-done.13 = bf16[512,512]{1,0:T(8,128)(2,1)S(1)} collective-permute-done((bf16[512,512]{1,0:T(8,128)(2,1)S(1)}, bf16[512,512]{1,0:T(8,128)(2,1)S(1)}, u32[]{:S(2)}, u32[]{:S(2)}) %collective-permute-start.13) | collective-permute-done | bytes 524320 | tf_op jit(solution)/shard_map/ppermute | solution.py:29
  125.6 8.9 %all-to-all-start.2 = ((bf16[32,16,512]{2,1,0:T(8,128)(2,1)}), bf16[32,16,512]{2,1,0:T(8,128)(2,1)S(1)}, u32[]{:S(2)}, u32[]{:S(2)}) async-start(bf16[32,16,512]{2,1,0:T(8,128)(2,1)} %bitcast.9), calls=%async_computation.2 | async-start | bytes 1048576 | tf_op jit(solution)/shard_map/all_to_all | solution.py:39
  136.0 3.6 %collective-permute-done.14 = f32[16,512]{1,0:T(8,128)S(1)} collective-permute-done((f32[16,512]{1,0:T(8,128)S(1)}, f32[16,512]{1,0:T(8,128)S(1)}, u32[]{:S(2)}, u32[]{:S(2)}) %collective-permute-start.14) | collective-permute-done | bytes 32800 | tf_op jit(solution)/shard_map/ppermute | solution.py:29
  139.6 2.2 %collective-permute-start.15 = (f32[16,512]{1,0:T(8,128)S(1)}, f32[16,512]{1,0:T(8,128)S(1)}, u32[]{:S(2)}, u32[]{:S(2)}) collective-permute-start(f32[16,512]{1,0:T(8,128)S(1)} %add.22), channel_id=1, source_target_pairs={{0,2},{1,3},{2,0},{3,1},{128,130},{129,131},{130,128},{131,129},{4... | collective-permute-start | bytes 98312 | tf_op jit(solution)/shard_map/ppermute | solution.py:29
  141.8 3.2 %collective-permute-done.15 = f32[16,512]{1,0:T(8,128)S(1)} collective-permute-done((f32[16,512]{1,0:T(8,128)S(1)}, f32[16,512]{1,0:T(8,128)S(1)}, u32[]{:S(2)}, u32[]{:S(2)}) %collective-permute-start.15) | collective-permute-done | bytes 32800 | tf_op jit(solution)/shard_map/ppermute | solution.py:29
  146.3 6.2 %all-to-all-done.2 = bf16[32,16,512]{2,1,0:T(8,128)(2,1)S(1)} async-done(((bf16[32,16,512]{2,1,0:T(8,128)(2,1)}), bf16[32,16,512]{2,1,0:T(8,128)(2,1)S(1)}, u32[]{:S(2)}, u32[]{:S(2)}) %all-to-all-start.2) | async-done | bytes 524320 | tf_op jit(solution)/shard_map/all_to_all | solution.py:39
  152.5 16.7 %all_to_all.34 = bf16[32,8,512]{2,1,0:T(8,128)(2,1)S(1)} all-to-all(bf16[32,8,512]{2,1,0:T(8,128)(2,1)S(1)} %broadcast_in_dim.24), channel_id=1, replica_groups=mesh['grp'=2,'dp'=32,'mp'=4] {'dp'}, dimensions={0} | all-to-all | bytes 524288 | tf_op jit(solution)/shard_map/all_to_all | solution.py:39
  (70 shorter events, 30.1 us)
Async XLA Ops:
  0.6 21.1 %copy-start = (bf16[2048,512]{1,0:T(8,128)(2,1)S(1)}, bf16[2048,512]{1,0:T(8,128)(2,1)}, u32[]{:S(2)}) copy-start(bf16[2048,512]{1,0:T(8,128)(2,1)} %param.15) | copy-start | bytes 6291460
  0.7 50.2 %collective-permute-start = (bf16[4096,256]{1,0:T(8,128)(2,1)}, bf16[4096,256]{1,0:T(8,128)(2,1)}, u32[]{:S(2)}, u32[]{:S(2)}) collective-permute-start(bf16[4096,256]{1,0:T(8,128)(2,1)} %refs_2_.3), channel_id=1, source_target_pairs={{0,128},{1,129},{2,130},{3,131},{128,0},{129,1},{130,2},{131,3},{4... | collective-permute-start | bytes 6291464 | tf_op jit(solution)/shard_map/ppermute | solution.py:29
  10.2 39.6 %all-to-all-start = ((bf16[32,128,128]{2,1,0:T(8,128)(2,1)}), bf16[32,128,128]{2,1,0:T(8,128)(2,1)S(1)}, u32[]{:S(2)}, u32[]{:S(2)}) async-start(bf16[32,128,128]{2,1,0:T(8,128)(2,1)} %bitcast.5), calls=%async_computation | async-start | bytes 2097152 | tf_op jit(solution)/shard_map/all_to_all | solution.py:232
  21.6 29.7 %copy-start.10 = (s32[32]{0:T(128)S(1)}, s32[32]{0:T(128)}, u32[]{:S(2)}) copy-start(s32[32]{0:T(128)} %param.12) | copy-start | bytes 388
  21.6 36.1 %collective-permute-start.4 = (bf16[4096,256]{1,0:T(8,128)(2,1)}, bf16[4096,256]{1,0:T(8,128)(2,1)}, u32[]{:S(2)}, u32[]{:S(2)}) collective-permute-start(bf16[4096,256]{1,0:T(8,128)(2,1)} %refs_2_.3), channel_id=1, source_target_pairs={{0,1},{1,0},{2,3},{3,2},{128,129},{129,128},{130,131},{131,130},{4... | collective-permute-start | bytes 6291464 | tf_op jit(solution)/shard_map/ppermute | solution.py:29
  50.8 32.4 %collective-permute-start.7 = (bf16[4096,256]{1,0:T(8,128)(2,1)}, bf16[4096,256]{1,0:T(8,128)(2,1)S(1)}, u32[]{:S(2)}, u32[]{:S(2)}) collective-permute-start(bf16[4096,256]{1,0:T(8,128)(2,1)} %collective-permute-done.refs_2_), channel_id=1, source_target_pairs={{0,1},{1,0},{2,3},{3,2},{128,129},{129,128},{130,131},{131,130},{4... | collective-permute-start | bytes 6291464 | tf_op jit(solution)/shard_map/ppermute | solution.py:29
  50.8 5.5 %collective-permute-start.3 = (bf16[512,512]{1,0:T(8,128)(2,1)}, bf16[512,512]{1,0:T(8,128)(2,1)S(1)}, u32[]{:S(2)}, u32[]{:S(2)}) collective-permute-start(bf16[512,512]{1,0:T(8,128)(2,1)} %pad_maximum_fusion.refs_0_), channel_id=1, source_target_pairs={{0,1},{1,0},{2,3},{3,2},{128,129},{129,128},{130,131},{131,130},{4... | collective-permute-start | bytes 1572872 | tf_op jit(solution)/shard_map/ppermute | solution.py:29
  53.5 7.0 %copy-start.9 = (bf16[4096,512]{1,0:T(8,128)(2,1)S(1)}, bf16[4096,512]{1,0:T(8,128)(2,1)}, u32[]{:S(2)}) copy-start(bf16[4096,512]{1,0:T(8,128)(2,1)} %param.16) | copy-start | bytes 12582916
  53.5 26.6 %collective-permute-start.1 = (bf16[128,4096]{1,0:T(8,128)(2,1)S(1)}, bf16[128,4096]{1,0:T(8,128)(2,1)}, u32[]{:S(2)}, u32[]{:S(2)}) collective-permute-start(bf16[128,4096]{1,0:T(8,128)(2,1)S(1)} %arrange.1.features_ref.refs_0_), channel_id=1, source_target_pairs={{0,130},{1,131},{2,128},{3,129},{128,2},{129,3},{130,0},{131,1},{4... | collective-permute-start | bytes 3145736 | tf_op jit(solution)/shard_map/ppermute | solution.py:29
  55.7 15.1 %collective-permute-start.2 = (bf16[512,512]{1,0:T(8,128)(2,1)}, bf16[512,512]{1,0:T(8,128)(2,1)S(1)}, u32[]{:S(2)}, u32[]{:S(2)}) collective-permute-start(bf16[512,512]{1,0:T(8,128)(2,1)} %pad_maximum_fusion.refs_0_), channel_id=1, source_target_pairs={{0,128},{1,129},{2,130},{3,131},{128,0},{129,1},{130,2},{131,3},{4... | collective-permute-start | bytes 1572872 | tf_op jit(solution)/shard_map/ppermute | solution.py:29
  56.3 36.9 %collective-permute-start.9 = (bf16[128,4096]{1,0:T(8,128)(2,1)S(1)}, bf16[128,4096]{1,0:T(8,128)(2,1)S(1)}, u32[]{:S(2)}, u32[]{:S(2)}) collective-permute-start(bf16[128,4096]{1,0:T(8,128)(2,1)S(1)} %arrange.1.features_ref.refs_0_), channel_id=1, source_target_pairs={{0,128},{1,129},{2,130},{3,131},{128,0},{129,1},{130,2},{131,3},{4... | collective-permute-start | bytes 3145736 | tf_op jit(solution)/shard_map/ppermute | solution.py:29
  80.1 35.7 %collective-permute-start.5 = (bf16[128,4096]{1,0:T(8,128)(2,1)}, bf16[128,4096]{1,0:T(8,128)(2,1)}, u32[]{:S(2)}, u32[]{:S(2)}) collective-permute-start(bf16[128,4096]{1,0:T(8,128)(2,1)} %collective-permute-done.1.features_ref.refs_2_), channel_id=1, source_target_pairs={{0,128},{1,129},{2,130},{3,131},{128,0},{129,1},{130,2},{131,3},{4... | collective-permute-start | bytes 3145736 | tf_op jit(solution)/shard_map/ppermute | solution.py:29
  80.1 3.1 %collective-permute-start.6 = (bf16[512,512]{1,0:T(8,128)(2,1)S(1)}, bf16[512,512]{1,0:T(8,128)(2,1)S(1)}, u32[]{:S(2)}, u32[]{:S(2)}) collective-permute-start(bf16[512,512]{1,0:T(8,128)(2,1)S(1)} %collective-permute-done.2.refs_0_), channel_id=1, source_target_pairs={{0,1},{1,0},{2,3},{3,2},{128,129},{129,128},{130,131},{131,130},{4... | collective-permute-start | bytes 1572872 | tf_op jit(solution)/shard_map/ppermute | solution.py:29
  86.1 7.2 %collective-permute-start.8 = (bf16[128,512]{1,0:T(8,128)(2,1)S(1)}, bf16[128,512]{1,0:T(8,128)(2,1)S(1)}, u32[]{:S(2)}, u32[]{:S(2)}) collective-permute-start(bf16[128,512]{1,0:T(8,128)(2,1)S(1)} %teacher.6), channel_id=1, source_target_pairs={{0,130},{1,131},{2,128},{3,129},{128,2},{129,3},{130,0},{131,1},{4... | collective-permute-start | bytes 393224 | tf_op jit(solution)/shard_map/ppermute | solution.py:29
  95.0 30.6 %all-to-all-start.1 = ((bf16[32,16,512]{2,1,0:T(8,128)(2,1)}), bf16[32,16,512]{2,1,0:T(8,128)(2,1)}, u32[]{:S(2)}, u32[]{:S(2)}) async-start(bf16[32,16,512]{2,1,0:T(8,128)(2,1)} %bitcast.25), calls=%async_computation.1 | async-start | bytes 1048576 | tf_op jit(solution)/shard_map/all_to_all | solution.py:39
  104.7 13.8 %collective-permute-start.10 = (bf16[128,512]{1,0:T(8,128)(2,1)S(1)}, bf16[128,512]{1,0:T(8,128)(2,1)S(1)}, u32[]{:S(2)}, u32[]{:S(2)}) collective-permute-start(bf16[128,512]{1,0:T(8,128)(2,1)S(1)} %get-tuple-element.40.refs_0_), channel_id=1, source_target_pairs={{0,128},{1,129},{2,130},{3,131},{128,0},{129,1},{130,2},{131,3},{4... | collective-permute-start | bytes 393224 | tf_op jit(solution)/shard_map/ppermute | solution.py:29
  105.3 13.2 %collective-permute-start.11 = (bf16[128,512]{1,0:T(8,128)(2,1)S(1)}, bf16[128,512]{1,0:T(8,128)(2,1)S(1)}, u32[]{:S(2)}, u32[]{:S(2)}) collective-permute-start(bf16[128,512]{1,0:T(8,128)(2,1)S(1)} %get-tuple-element.40.refs_0_), channel_id=1, source_target_pairs={{0,130},{1,131},{2,128},{3,129},{128,2},{129,3},{130,0},{131,1},{4... | collective-permute-start | bytes 393224 | tf_op jit(solution)/shard_map/ppermute | solution.py:29
  107.6 13.1 %collective-permute-start.12 = (bf16[128,512]{1,0:T(8,128)(2,1)S(1)}, bf16[128,512]{1,0:T(8,128)(2,1)}, u32[]{:S(2)}, u32[]{:S(2)}) collective-permute-start(bf16[128,512]{1,0:T(8,128)(2,1)S(1)} %get-tuple-element.40.refs_0_), channel_id=1, source_target_pairs={{0,2},{1,3},{2,0},{3,1},{128,130},{129,131},{130,128},{131,129},{4... | collective-permute-start | bytes 393224 | tf_op jit(solution)/shard_map/ppermute | solution.py:29
  122.7 2.0 %collective-permute-start.13 = (bf16[512,512]{1,0:T(8,128)(2,1)S(1)}, bf16[512,512]{1,0:T(8,128)(2,1)S(1)}, u32[]{:S(2)}, u32[]{:S(2)}) collective-permute-start(bf16[512,512]{1,0:T(8,128)(2,1)S(1)} %get-tuple-element.42), channel_id=1, source_target_pairs={{0,1},{1,0},{2,3},{3,2},{128,129},{129,128},{130,131},{131,130},{4... | collective-permute-start | bytes 1572872 | tf_op jit(solution)/shard_map/ppermute | solution.py:29
  125.6 26.8 %all-to-all-start.2 = ((bf16[32,16,512]{2,1,0:T(8,128)(2,1)}), bf16[32,16,512]{2,1,0:T(8,128)(2,1)S(1)}, u32[]{:S(2)}, u32[]{:S(2)}) async-start(bf16[32,16,512]{2,1,0:T(8,128)(2,1)} %bitcast.9), calls=%async_computation.2 | async-start | bytes 1048576 | tf_op jit(solution)/shard_map/all_to_all | solution.py:39
  135.6 4.0 %collective-permute-start.14 = (f32[16,512]{1,0:T(8,128)S(1)}, f32[16,512]{1,0:T(8,128)S(1)}, u32[]{:S(2)}, u32[]{:S(2)}) collective-permute-start(f32[16,512]{1,0:T(8,128)S(1)} %convert_reduce_fusion.1), channel_id=1, source_target_pairs={{0,128},{1,129},{2,130},{3,131},{128,0},{129,1},{130,2},{131,3},{4... | collective-permute-start | bytes 98312 | tf_op jit(solution)/shard_map/ppermute | solution.py:29
  139.6 5.4 %collective-permute-start.15 = (f32[16,512]{1,0:T(8,128)S(1)}, f32[16,512]{1,0:T(8,128)S(1)}, u32[]{:S(2)}, u32[]{:S(2)}) collective-permute-start(f32[16,512]{1,0:T(8,128)S(1)} %add.22), channel_id=1, source_target_pairs={{0,2},{1,3},{2,0},{3,1},{128,130},{129,131},{130,128},{131,129},{4... | collective-permute-start | bytes 98312 | tf_op jit(solution)/shard_map/ppermute | solution.py:29
  145.1 1.2 collective-permute-start.16
  169.2 1.5 collective-permute-start.17
  (8 other events, 17.3 us)

commit v4 on v3

--- a/solution.py
+++ b/solution.py
@@ -64,22 +64,48 @@
     )(order, averaged)
 
 
-def arrange_kernel(inverse_ref, arrived_ref, features_ref):
+def arrange_kernel(inverse_ref, spot_ref, arrived_ref, features_ref, half_ref):
     tables, _, width = arrived_ref.shape
     for column in range(tables):
         features_ref[:, column * width : (column + 1) * width] = arrived_ref[inverse_ref[column]]
-
-
-def arrange(arrived, inverse):
+    start = (1 - spot_ref[0]) * (tables // 2)
+    for column in range(tables // 2):
+        half_ref[:, column * width : (column + 1) * width] = arrived_ref[inverse_ref[start + column]]
+
+
+def arrange(arrived, inverse, spot):
     tables, rows, width = arrived.shape
     return pl.pallas_call(
         arrange_kernel,
-        out_shape=jax.ShapeDtypeStruct((rows, tables * width), arrived.dtype),
+        out_shape=tuple(
+            jax.ShapeDtypeStruct((rows, columns), arrived.dtype)
+            for columns in (tables * width, tables * width // 2)
+        ),
+        in_specs=[smem, smem, vmem],
+        out_specs=(vmem, vmem),
+        compiler_params=limit(6),
+        name="arrange",
+    )(inverse, spot, arrived)
+
+
+def half_kernel(spot_ref, features_ref, half_ref):
+    span = half_ref.shape[1]
+    start = (1 - spot_ref[0]) * span
+    for column in range(0, span, 128):
+        columns = pl.ds(pl.multiple_of(start + column, 128), 128)
+        half_ref[:, column : column + 128] = features_ref[:, columns]
+
+
+def near_half(spot, features):
+    return pl.pallas_call(
+        half_kernel,
+        out_shape=jax.ShapeDtypeStruct((features.shape[0], features.shape[1] // 2), features.dtype),
         in_specs=[smem, vmem],
         out_specs=vmem,
         compiler_params=limit(6),
-        name="arrange",
-    )(inverse, arrived)
+        cost_estimate=pl.CostEstimate(flops=0, bytes_accessed=0, transcendentals=0),
+        name="near_half",
+    )(spot, features)
 
 
 def teacher_kernel(features_ref, *refs):
@@ -144,12 +170,14 @@
 
 def turn_kernel(spot_ref, *refs):
     pieces, turned_ref = refs[:-1], refs[-1]
-    span = pieces[0].shape[1] // 2
-    start = spot_ref[0] * span
+    span = 4 * turned_ref.shape[1]
     high = spot_ref[1]
     for column in range(span // 128):
-        columns = pl.ds(pl.multiple_of(start + column * 128, 128), 128)
-        rows = jnp.concatenate([ref[:, columns] for ref in pieces], axis=0)
+        whole = pl.ds(pl.multiple_of(spot_ref[0] * span + column * 128, 128), 128)
+        half = slice(column * 128, (column + 1) * 128)
+        rows = jnp.concatenate(
+            [ref[:, half] if ref.shape[1] == span else ref[:, whole] for ref in pieces], axis=0
+        )
         for block in range(rows.shape[0] // 128):
             samples = slice(block * 128, (block + 1) * 128)
             turned = rows[samples].astype(jnp.float32).T
@@ -163,11 +191,11 @@
                     turned_ref[core, place : place + 16, samples] = kept[core * 16 : core * 16 + 16]
 
 
-def turn(spot, *pieces):
+def turn(spot, span, *pieces):
     samples = sum(piece.shape[0] for piece in pieces)
     return pl.pallas_call(
         turn_kernel,
-        out_shape=jax.ShapeDtypeStruct((2, pieces[0].shape[1] // 8, samples), jnp.bfloat16),
+        out_shape=jax.ShapeDtypeStruct((2, span // 4, samples), jnp.bfloat16),
         in_specs=[smem] + [vmem] * len(pieces),
         out_specs=vmem,
         compiler_params=limit(8),
@@ -239,10 +267,11 @@
     core_joined = swap(joined, CORE)
     arrived, near_w1, joined = tie(arrived, near_w1, joined)
 
-    own = arrange(arrived, inverse)
+    own, half = arrange(arrived, inverse, spot)
+    span = half.shape[1]
     near_core_w1 = swap(near_w1, CORE)
     far = swap(own, FAR)
-    near = swap(own, NEAR)
+    near = swap(half, NEAR)
 
     student_pre = dot(own, student_w1)
     student_hidden = jax.nn.relu(student_pre).astype(jnp.bfloat16)
@@ -255,11 +284,11 @@
     partial = teacher(far, *chip)
     partial = teacher(far, *next_chip, partial, kept=jnp.bfloat16)
     there = swap(partial, FAR)
-    opposite = swap(far, NEAR)
+    opposite = swap(near_half(spot, far), NEAR)
     later_own, _ = tie(own, partial)
     here = teacher(later_own, *next_chip, here)
     there, here, near = tie(there, here, near)
-    early = turn(spot, own, near, far)
+    early = turn(spot, span, own, near, far)
 
     devices = lax.axis_size("grp") * lax.axis_size("dp") * lax.axis_size("mp")
     grad_scale = 8192.0 / (samples * devices * outer)
@@ -268,7 +297,7 @@
     )
     grads = [grad] + [swap(grad, mask) for mask in (NEAR, FAR, OPPOSITE)]
     opposite, early = tie(opposite, early)
-    late = turn(spot, opposite)
+    late = turn(spot, span, opposite)
 
     second = across(second)
     mine, other = gradients(spot, early, late, grads)

time: 174 us -> 170 us (0.977)
  waiting for transfers between devices: 70.2 us -> 64.1 us
    ppermute x18, waiting for transfers between devices: 38.8 us -> 29.7 us  [swap(): lax.ppermute(values, LINE, [(index, index ^ mask) for index in range(8)])]
    all_to_all x2, waiting for transfers between devices: 6.16 us -> 9.11 us  [across(): return lax.all_to_all(values, 'dp', split_axis=0, concat_axis=0, tiled=True)]
    pallas_call x3 -> x4, Pallas kernels: 4.06 us -> 4.81 us  [the longest x2 2.36 us: turn(): pl.pallas_call(turn_kernel, out_shape=jax.ShapeDtypeStruct((2, span // 4,...]
    unnamed x22 -> x24, local copies, waits for them, and re-layouts: 4.51 us -> 5.09 us
  transfers between devices with their start and end apart: 21 -> 21, of which waited for: 14 -> 13; matrix products, arithmetic and copies ran while one was open for 5% -> 6% of each run, Pallas kernels for 14% -> 15%
where the time goes in v4:
time: 170 us; the launch traced here: 168 us
  waiting for transfers between devices  64.1 us (38%)
  starting transfers between devices  44.9 us (26%)
  Pallas kernels  25.1 us (15%)
  blocking collectives  16.7 us (10%)
  other arithmetic  7.81 us (5%)
  local copies, waits for them, and re-layouts  5.11 us (3%)
  matrix products  2.87 us (2%)
    ppermute x18, waiting for transfers between devices, swap(): lax.ppermute(values, LINE, [(index, index ^ mask) for index in range(8)])  29.7 us
    all_to_all x1, waiting for transfers between devices, shards(): lax.all_to_all(ordered.reshape(tables, samples, width), 'dp', split_axis=...  25.2 us
    all_to_all x2, starting transfers between devices, across(): return lax.all_to_all(values, 'dp', split_axis=0, concat_axis=0, tiled=True)  17 us
    all_to_all x1, blocking collectives, across(): return lax.all_to_all(values, 'dp', split_axis=0, concat_axis=0, tiled=True)  16.7 us
    ppermute x18, starting transfers between devices, swap(): lax.ppermute(values, LINE, [(index, index ^ mask) for index in range(8)])  16.6 us
    pallas_call x4, Pallas kernels, teacher(): pl.pallas_call(teacher_kernel, out_shape=jax.ShapeDtypeStruct((features.s...  12.4 us
    all_to_all x1, starting transfers between devices, shards(): lax.all_to_all(ordered.reshape(tables, samples, width), 'dp', split_axis=...  11.4 us
    all_to_all x2, waiting for transfers between devices, across(): return lax.all_to_all(values, 'dp', split_axis=0, concat_axis=0, tiled=True)  9.11 us
  transfers between devices with their start and end apart: 21, of which 13 were waited for; matrix products, arithmetic and copies ran while one was open for 6% of the time, Pallas kernels for 15%

profile of v4, /device:TPU:32, one launch (start us, length us, event | category | flops | bytes accessed | tf_op | source)
XLA Modules:
  0.0 167.5 jit_solution(7487998701396631244)
XLA Ops:
  3.0 1.8 %convert_divide_fusion.averaged_ref = f32[4096,128]{1,0:T(8,128)S(1)} fusion(bf16[1,1,4096,128]{3,2,1,0:T(8,128)(2,1)} %param.9, f32[4096]{0:T(1024)S(1)} %bitcast.26), kind=kLoop, calls=%fused_computation | loop fusion | flops 1048576 | bytes 3162112 | tf_op jit(solution)/shard_map/div | solution.py:258
  4.8 5.5 %take_rows.1 = bf16[4096,128]{1,0:T(8,128)(2,1)} custom-call(s32[1,4096]{1,0:T(1,128)S(1)} %copy-done.9, f32[4096,128]{1,0:T(8,128)S(1)} %convert_divide_fusion.averaged_ref), custom_call_target="tpu_custom_call" | custom-call | tf_op jit(solution)/shard_map/take_rows/pallas_call | solution.py:57
  10.2 11.4 %all-to-all-start = ((bf16[32,128,128]{2,1,0:T(8,128)(2,1)}), bf16[32,128,128]{2,1,0:T(8,128)(2,1)S(1)}, u32[]{:S(2)}, u32[]{:S(2)}) async-start(bf16[32,128,128]{2,1,0:T(8,128)(2,1)} %bitcast.5), calls=%async_computation | async-start | bytes 2097152 | tf_op jit(solution)/shard_map/all_to_all | solution.py:260
  21.7 1.9 %fusion = (bf16[256,512]{1,0:T(8,128)(2,1)S(1)}, f32[256,512]{1,0:T(8,128)S(1)}) fusion(bf16[256,2048]{1,0:T(8,128)(2,1)} %param.14, bf16[2048,512]{1,0:T(8,128)(2,1)S(1)} %copy-done), kind=kOutput, calls=%fused_computation.14 | convolution fusion | flops 537001984 | bytes 3932160 | tf_op jit(solution)/shard_map/dot_general | solution.py:25
  24.6 25.2 %all-to-all-done.arrived_ref = bf16[32,128,128]{2,1,0:T(8,128)(2,1)S(1)} async-done(((bf16[32,128,128]{2,1,0:T(8,128)(2,1)}), bf16[32,128,128]{2,1,0:T(8,128)(2,1)S(1)}, u32[]{:S(2)}, u32[]{:S(2)}) %all-to-all-start) | async-done | bytes 1048608 | tf_op jit(solution)/shard_map/all_to_all | solution.py:260
  51.5 2.2 %collective-permute-start.1 = (bf16[128,4096]{1,0:T(8,128)(2,1)S(1)}, bf16[128,4096]{1,0:T(8,128)(2,1)S(1)}, u32[]{:S(2)}, u32[]{:S(2)}) collective-permute-start(bf16[128,4096]{1,0:T(8,128)(2,1)S(1)} %get-tuple-element.35.features_ref.refs_0_), channel_id=1, source_target_pairs={{0,130},{1,131},{2,128},{3,129},{128,2},{129,3},{130,0},{131,1},{4... | collective-permute-start | bytes 3145736 | tf_op jit(solution)/shard_map/ppermute | solution.py:29
  56.7 3.0 %teacher.4.refs_4_ = f32[128,512]{1,0:T(8,128)S(1)} custom-call(bf16[128,4096]{1,0:T(8,128)(2,1)S(1)} %get-tuple-element.35.features_ref.refs_0_, bf16[512,512]{1,0:T(8,128)(2,1)} %pad_maximum_fusion.refs_0_, bf16[512,512]{1,0:T(8,128)(2,1)} %collective-permute-done.3.refs_1_, bf16[4096,256]{1,0:T(8,128)(2,1)S(1)} %copy-done.3, ...), custom_call_target="tpu_custom_call" | custom-call | tf_op jit(solution)/shard_map/teacher/pallas_call | solution.py:123
  61.1 6.4 %collective-permute-done.2.refs_0_ = bf16[512,512]{1,0:T(8,128)(2,1)S(1)} collective-permute-done((bf16[512,512]{1,0:T(8,128)(2,1)}, bf16[512,512]{1,0:T(8,128)(2,1)S(1)}, u32[]{:S(2)}, u32[]{:S(2)}) %collective-permute-start.2) | collective-permute-done | bytes 524320 | tf_op jit(solution)/shard_map/ppermute | solution.py:29
  67.5 10.4 %collective-permute-done.1.features_ref.refs_2_ = bf16[128,4096]{1,0:T(8,128)(2,1)S(1)} collective-permute-done((bf16[128,4096]{1,0:T(8,128)(2,1)S(1)}, bf16[128,4096]{1,0:T(8,128)(2,1)S(1)}, u32[]{:S(2)}, u32[]{:S(2)}) %collective-permute-start.1) | collective-permute-done | bytes 1048608 | tf_op jit(solution)/shard_map/ppermute | solution.py:29
  79.4 2.0 %collective-permute-start.5 = (bf16[128,2048]{1,0:T(8,128)(2,1)}, bf16[128,2048]{1,0:T(8,128)(2,1)}, u32[]{:S(2)}, u32[]{:S(2)}) collective-permute-start(bf16[128,2048]{1,0:T(8,128)(2,1)} %near_half.1), channel_id=1, source_target_pairs={{0,128},{1,129},{2,130},{3,131},{128,0},{129,1},{130,2},{131,3},{4... | collective-permute-start | bytes 1572872 | tf_op jit(solution)/shard_map/ppermute | solution.py:29
  81.4 2.9 %teacher.5.refs_4_ = f32[128,512]{1,0:T(8,128)S(1)} custom-call(bf16[128,4096]{1,0:T(8,128)(2,1)S(1)} %collective-permute-done.1.features_ref.refs_2_, bf16[512,512]{1,0:T(8,128)(2,1)} %pad_maximum_fusion.refs_0_, bf16[512,512]{1,0:T(8,128)(2,1)} %collective-permute-done.3.refs_1_, bf16[4096,256]{1,0:T(8,128)(2,1)S(1)} %copy-done.4, ...), custom_call_target="tpu_custom_call" | custom-call | tf_op jit(solution)/shard_map/teacher/pallas_call | solution.py:123
  84.4 3.2 %teacher.6 = bf16[128,512]{1,0:T(8,128)(2,1)S(1)} custom-call(bf16[128,4096]{1,0:T(8,128)(2,1)S(1)} %collective-permute-done.1.features_ref.refs_2_, bf16[512,512]{1,0:T(8,128)(2,1)S(1)} %collective-permute-done.2.refs_0_, bf16[512,512]{1,0:T(8,128)(2,1)S(1)} %collective-permute-done.6.refs_1_, bf16[4096,256]{1,0:T(8,128)(2,1)} %collective-permute-done.refs_2_, ...), custom_call_target="tpu_custom_call" | custom-call | tf_op jit(solution)/shard_map/teacher/pallas_call | solution.py:123
  87.6 2.2 %collective-permute-start.8 = (bf16[128,512]{1,0:T(8,128)(2,1)S(1)}, bf16[128,512]{1,0:T(8,128)(2,1)S(1)}, u32[]{:S(2)}, u32[]{:S(2)}) collective-permute-start(bf16[128,512]{1,0:T(8,128)(2,1)S(1)} %teacher.6), channel_id=1, source_target_pairs={{0,130},{1,131},{2,128},{3,129},{128,2},{129,3},{130,0},{131,1},{4... | collective-permute-start | bytes 393224 | tf_op jit(solution)/shard_map/ppermute | solution.py:29
  89.8 3.2 %teacher.7.refs_1_ = f32[128,512]{1,0:T(8,128)S(1)} custom-call(bf16[128,4096]{1,0:T(8,128)(2,1)S(1)} %get-tuple-element.35.features_ref.refs_0_, bf16[512,512]{1,0:T(8,128)(2,1)S(1)} %collective-permute-done.2.refs_0_, bf16[512,512]{1,0:T(8,128)(2,1)S(1)} %collective-permute-done.6.refs_1_, bf16[4096,256]{1,0:T(8,128)(2,1)} %collective-permute-done.refs_2_, ...), custom_call_target="tpu_custom_call" | custom-call | tf_op jit(solution)/shard_map/teacher/pallas_call | solution.py:123
  96.0 10.2 %all-to-all-start.1 = ((bf16[32,16,512]{2,1,0:T(8,128)(2,1)}), bf16[32,16,512]{2,1,0:T(8,128)(2,1)}, u32[]{:S(2)}, u32[]{:S(2)}) async-start(bf16[32,16,512]{2,1,0:T(8,128)(2,1)} %bitcast.25), calls=%async_computation.1 | async-start | bytes 1048576 | tf_op jit(solution)/shard_map/all_to_all | solution.py:39
  106.3 2.8 %collective-permute-start.11 = (bf16[128,512]{1,0:T(8,128)(2,1)S(1)}, bf16[128,512]{1,0:T(8,128)(2,1)S(1)}, u32[]{:S(2)}, u32[]{:S(2)}) collective-permute-start(bf16[128,512]{1,0:T(8,128)(2,1)S(1)} %get-tuple-element.44.refs_0_), channel_id=1, source_target_pairs={{0,130},{1,131},{2,128},{3,129},{128,2},{129,3},{130,0},{131,1},{4... | collective-permute-start | bytes 393224 | tf_op jit(solution)/shard_map/ppermute | solution.py:29
  117.2 1.9 %collective-permute-done.13 = bf16[512,512]{1,0:T(8,128)(2,1)S(1)} collective-permute-done((bf16[512,512]{1,0:T(8,128)(2,1)S(1)}, bf16[512,512]{1,0:T(8,128)(2,1)S(1)}, u32[]{:S(2)}, u32[]{:S(2)}) %collective-permute-start.13) | collective-permute-done | bytes 524320 | tf_op jit(solution)/shard_map/ppermute | solution.py:29
  120.1 3.0 %all-to-all-done.1 = bf16[32,16,512]{2,1,0:T(8,128)(2,1)} async-done(((bf16[32,16,512]{2,1,0:T(8,128)(2,1)}), bf16[32,16,512]{2,1,0:T(8,128)(2,1)}, u32[]{:S(2)}, u32[]{:S(2)}) %all-to-all-start.1) | async-done | bytes 524320 | tf_op jit(solution)/shard_map/all_to_all | solution.py:39
  123.1 6.8 %all-to-all-start.2 = ((bf16[32,16,512]{2,1,0:T(8,128)(2,1)}), bf16[32,16,512]{2,1,0:T(8,128)(2,1)S(1)}, u32[]{:S(2)}, u32[]{:S(2)}) async-start(bf16[32,16,512]{2,1,0:T(8,128)(2,1)} %bitcast.9), calls=%async_computation.2 | async-start | bytes 1048576 | tf_op jit(solution)/shard_map/all_to_all | solution.py:39
  132.4 2.7 %collective-permute-done.14 = f32[16,512]{1,0:T(8,128)S(1)} collective-permute-done((f32[16,512]{1,0:T(8,128)S(1)}, f32[16,512]{1,0:T(8,128)S(1)}, u32[]{:S(2)}, u32[]{:S(2)}) %collective-permute-start.14) | collective-permute-done | bytes 32800 | tf_op jit(solution)/shard_map/ppermute | solution.py:29
  135.1 1.7 collective-permute-start.15
  136.7 3.8 %collective-permute-done.15 = f32[16,512]{1,0:T(8,128)S(1)} collective-permute-done((f32[16,512]{1,0:T(8,128)S(1)}, f32[16,512]{1,0:T(8,128)S(1)}, u32[]{:S(2)}, u32[]{:S(2)}) %collective-permute-start.15) | collective-permute-done | bytes 32800 | tf_op jit(solution)/shard_map/ppermute | solution.py:29
  141.7 6.2 %all-to-all-done.2 = bf16[32,16,512]{2,1,0:T(8,128)(2,1)S(1)} async-done(((bf16[32,16,512]{2,1,0:T(8,128)(2,1)}), bf16[32,16,512]{2,1,0:T(8,128)(2,1)S(1)}, u32[]{:S(2)}, u32[]{:S(2)}) %all-to-all-start.2) | async-done | bytes 524320 | tf_op jit(solution)/shard_map/all_to_all | solution.py:39
  147.9 16.7 %all_to_all.34 = bf16[32,8,512]{2,1,0:T(8,128)(2,1)S(1)} all-to-all(bf16[32,8,512]{2,1,0:T(8,128)(2,1)S(1)} %broadcast_in_dim.24), channel_id=1, replica_groups=mesh['grp'=2,'dp'=32,'mp'=4] {'dp'}, dimensions={0} | all-to-all | bytes 524288 | tf_op jit(solution)/shard_map/all_to_all | solution.py:39
  (73 shorter events, 29.6 us)
Async XLA Ops:
  0.6 21.1 %copy-start = (bf16[2048,512]{1,0:T(8,128)(2,1)S(1)}, bf16[2048,512]{1,0:T(8,128)(2,1)}, u32[]{:S(2)}) copy-start(bf16[2048,512]{1,0:T(8,128)(2,1)} %param.15) | copy-start | bytes 6291460
  0.7 49.2 %collective-permute-start = (bf16[4096,256]{1,0:T(8,128)(2,1)}, bf16[4096,256]{1,0:T(8,128)(2,1)}, u32[]{:S(2)}, u32[]{:S(2)}) collective-permute-start(bf16[4096,256]{1,0:T(8,128)(2,1)} %refs_2_.3), channel_id=1, source_target_pairs={{0,128},{1,129},{2,130},{3,131},{128,0},{129,1},{130,2},{131,3},{4... | collective-permute-start | bytes 6291464 | tf_op jit(solution)/shard_map/ppermute | solution.py:29
  10.2 39.6 %all-to-all-start = ((bf16[32,128,128]{2,1,0:T(8,128)(2,1)}), bf16[32,128,128]{2,1,0:T(8,128)(2,1)S(1)}, u32[]{:S(2)}, u32[]{:S(2)}) async-start(bf16[32,128,128]{2,1,0:T(8,128)(2,1)} %bitcast.5), calls=%async_computation | async-start | bytes 2097152 | tf_op jit(solution)/shard_map/all_to_all | solution.py:260
  21.6 28.8 %copy-start.11 = (s32[32]{0:T(128)S(1)}, s32[32]{0:T(128)}, u32[]{:S(2)}) copy-start(s32[32]{0:T(128)} %param.12) | copy-start | bytes 388
  21.6 33.5 %collective-permute-start.4 = (bf16[4096,256]{1,0:T(8,128)(2,1)}, bf16[4096,256]{1,0:T(8,128)(2,1)}, u32[]{:S(2)}, u32[]{:S(2)}) collective-permute-start(bf16[4096,256]{1,0:T(8,128)(2,1)} %refs_2_.3), channel_id=1, source_target_pairs={{0,1},{1,0},{2,3},{3,2},{128,129},{129,128},{130,131},{131,130},{4... | collective-permute-start | bytes 6291464 | tf_op jit(solution)/shard_map/ppermute | solution.py:29
  49.8 34.5 %collective-permute-start.7 = (bf16[4096,256]{1,0:T(8,128)(2,1)}, bf16[4096,256]{1,0:T(8,128)(2,1)}, u32[]{:S(2)}, u32[]{:S(2)}) collective-permute-start(bf16[4096,256]{1,0:T(8,128)(2,1)} %collective-permute-done.refs_2_), channel_id=1, source_target_pairs={{0,1},{1,0},{2,3},{3,2},{128,129},{129,128},{130,131},{131,130},{4... | collective-permute-start | bytes 6291464 | tf_op jit(solution)/shard_map/ppermute | solution.py:29
  49.9 5.2 %collective-permute-start.3 = (bf16[512,512]{1,0:T(8,128)(2,1)}, bf16[512,512]{1,0:T(8,128)(2,1)}, u32[]{:S(2)}, u32[]{:S(2)}) collective-permute-start(bf16[512,512]{1,0:T(8,128)(2,1)} %pad_maximum_fusion.refs_0_), channel_id=1, source_target_pairs={{0,1},{1,0},{2,3},{3,2},{128,129},{129,128},{130,131},{131,130},{4... | collective-permute-start | bytes 1572872 | tf_op jit(solution)/shard_map/ppermute | solution.py:29
  51.5 38.3 %copy-start.1 = (bf16[128,4096]{1,0:T(8,128)(2,1)}, bf16[128,4096]{1,0:T(8,128)(2,1)S(1)}, u32[]{:S(2)}) copy-start(bf16[128,4096]{1,0:T(8,128)(2,1)S(1)} %get-tuple-element.35.features_ref.refs_0_) | copy-start | bytes 3145732
  51.5 26.4 %collective-permute-start.1 = (bf16[128,4096]{1,0:T(8,128)(2,1)S(1)}, bf16[128,4096]{1,0:T(8,128)(2,1)S(1)}, u32[]{:S(2)}, u32[]{:S(2)}) collective-permute-start(bf16[128,4096]{1,0:T(8,128)(2,1)S(1)} %get-tuple-element.35.features_ref.refs_0_), channel_id=1, source_target_pairs={{0,130},{1,131},{2,128},{3,129},{128,2},{129,3},{130,0},{131,1},{4... | collective-permute-start | bytes 3145736 | tf_op jit(solution)/shard_map/ppermute | solution.py:29
  53.7 13.8 %collective-permute-start.2 = (bf16[512,512]{1,0:T(8,128)(2,1)}, bf16[512,512]{1,0:T(8,128)(2,1)S(1)}, u32[]{:S(2)}, u32[]{:S(2)}) collective-permute-start(bf16[512,512]{1,0:T(8,128)(2,1)} %pad_maximum_fusion.refs_0_), channel_id=1, source_target_pairs={{0,128},{1,129},{2,130},{3,131},{128,0},{129,1},{130,2},{131,3},{4... | collective-permute-start | bytes 1572872 | tf_op jit(solution)/shard_map/ppermute | solution.py:29
  77.9 6.5 %collective-permute-start.6 = (bf16[512,512]{1,0:T(8,128)(2,1)S(1)}, bf16[512,512]{1,0:T(8,128)(2,1)S(1)}, u32[]{:S(2)}, u32[]{:S(2)}) collective-permute-start(bf16[512,512]{1,0:T(8,128)(2,1)S(1)} %collective-permute-done.2.refs_0_), channel_id=1, source_target_pairs={{0,1},{1,0},{2,3},{3,2},{128,129},{129,128},{130,131},{131,130},{4... | collective-permute-start | bytes 1572872 | tf_op jit(solution)/shard_map/ppermute | solution.py:29
  77.9 15.1 %collective-permute-start.9 = (bf16[128,2048]{1,0:T(8,128)(2,1)S(1)}, bf16[128,2048]{1,0:T(8,128)(2,1)S(1)}, u32[]{:S(2)}, u32[]{:S(2)}) collective-permute-start(bf16[128,2048]{1,0:T(8,128)(2,1)S(1)} %get-tuple-element.37), channel_id=1, source_target_pairs={{0,128},{1,129},{2,130},{3,131},{128,0},{129,1},{130,2},{131,3},{4... | collective-permute-start | bytes 1572872 | tf_op jit(solution)/shard_map/ppermute | solution.py:29
  79.4 34.4 %collective-permute-start.5 = (bf16[128,2048]{1,0:T(8,128)(2,1)}, bf16[128,2048]{1,0:T(8,128)(2,1)}, u32[]{:S(2)}, u32[]{:S(2)}) collective-permute-start(bf16[128,2048]{1,0:T(8,128)(2,1)} %near_half.1), channel_id=1, source_target_pairs={{0,128},{1,129},{2,130},{3,131},{128,0},{129,1},{130,2},{131,3},{4... | collective-permute-start | bytes 1572872 | tf_op jit(solution)/shard_map/ppermute | solution.py:29
  87.6 6.6 %collective-permute-start.8 = (bf16[128,512]{1,0:T(8,128)(2,1)S(1)}, bf16[128,512]{1,0:T(8,128)(2,1)S(1)}, u32[]{:S(2)}, u32[]{:S(2)}) collective-permute-start(bf16[128,512]{1,0:T(8,128)(2,1)S(1)} %teacher.6), channel_id=1, source_target_pairs={{0,130},{1,131},{2,128},{3,129},{128,2},{129,3},{130,0},{131,1},{4... | collective-permute-start | bytes 393224 | tf_op jit(solution)/shard_map/ppermute | solution.py:29
  96.0 27.1 %all-to-all-start.1 = ((bf16[32,16,512]{2,1,0:T(8,128)(2,1)}), bf16[32,16,512]{2,1,0:T(8,128)(2,1)}, u32[]{:S(2)}, u32[]{:S(2)}) async-start(bf16[32,16,512]{2,1,0:T(8,128)(2,1)} %bitcast.25), calls=%async_computation.1 | async-start | bytes 1048576 | tf_op jit(solution)/shard_map/all_to_all | solution.py:39
  106.2 8.9 %collective-permute-start.10 = (bf16[128,512]{1,0:T(8,128)(2,1)S(1)}, bf16[128,512]{1,0:T(8,128)(2,1)S(1)}, u32[]{:S(2)}, u32[]{:S(2)}) collective-permute-start(bf16[128,512]{1,0:T(8,128)(2,1)S(1)} %get-tuple-element.44.refs_0_), channel_id=1, source_target_pairs={{0,128},{1,129},{2,130},{3,131},{128,0},{129,1},{130,2},{131,3},{4... | collective-permute-start | bytes 393224 | tf_op jit(solution)/shard_map/ppermute | solution.py:29
  106.3 8.9 %collective-permute-start.11 = (bf16[128,512]{1,0:T(8,128)(2,1)S(1)}, bf16[128,512]{1,0:T(8,128)(2,1)S(1)}, u32[]{:S(2)}, u32[]{:S(2)}) collective-permute-start(bf16[128,512]{1,0:T(8,128)(2,1)S(1)} %get-tuple-element.44.refs_0_), channel_id=1, source_target_pairs={{0,130},{1,131},{2,128},{3,129},{128,2},{129,3},{130,0},{131,1},{4... | collective-permute-start | bytes 393224 | tf_op jit(solution)/shard_map/ppermute | solution.py:29
  109.1 6.6 %collective-permute-start.12 = (bf16[128,512]{1,0:T(8,128)(2,1)S(1)}, bf16[128,512]{1,0:T(8,128)(2,1)S(1)}, u32[]{:S(2)}, u32[]{:S(2)}) collective-permute-start(bf16[128,512]{1,0:T(8,128)(2,1)S(1)} %get-tuple-element.44.refs_0_), channel_id=1, source_target_pairs={{0,2},{1,3},{2,0},{3,1},{128,130},{129,131},{130,128},{131,129},{4... | collective-permute-start | bytes 393224 | tf_op jit(solution)/shard_map/ppermute | solution.py:29
  117.1 2.0 %collective-permute-start.13 = (bf16[512,512]{1,0:T(8,128)(2,1)S(1)}, bf16[512,512]{1,0:T(8,128)(2,1)S(1)}, u32[]{:S(2)}, u32[]{:S(2)}) collective-permute-start(bf16[512,512]{1,0:T(8,128)(2,1)S(1)} %get-tuple-element.46), channel_id=1, source_target_pairs={{0,1},{1,0},{2,3},{3,2},{128,129},{129,128},{130,131},{131,130},{4... | collective-permute-start | bytes 1572872 | tf_op jit(solution)/shard_map/ppermute | solution.py:29
  123.1 24.8 %all-to-all-start.2 = ((bf16[32,16,512]{2,1,0:T(8,128)(2,1)}), bf16[32,16,512]{2,1,0:T(8,128)(2,1)S(1)}, u32[]{:S(2)}, u32[]{:S(2)}) async-start(bf16[32,16,512]{2,1,0:T(8,128)(2,1)} %bitcast.9), calls=%async_computation.2 | async-start | bytes 1048576 | tf_op jit(solution)/shard_map/all_to_all | solution.py:39
  131.1 4.0 %collective-permute-start.14 = (f32[16,512]{1,0:T(8,128)S(1)}, f32[16,512]{1,0:T(8,128)S(1)}, u32[]{:S(2)}, u32[]{:S(2)}) collective-permute-start(f32[16,512]{1,0:T(8,128)S(1)} %convert_reduce_fusion.1), channel_id=1, source_target_pairs={{0,128},{1,129},{2,130},{3,131},{128,0},{129,1},{130,2},{131,3},{4... | collective-permute-start | bytes 98312 | tf_op jit(solution)/shard_map/ppermute | solution.py:29
  135.1 5.4 %collective-permute-start.15 = (f32[16,512]{1,0:T(8,128)S(1)}, f32[16,512]{1,0:T(8,128)S(1)}, u32[]{:S(2)}, u32[]{:S(2)}) collective-permute-start(f32[16,512]{1,0:T(8,128)S(1)} %add.22), channel_id=1, source_target_pairs={{0,2},{1,3},{2,0},{3,1},{128,130},{129,131},{130,128},{131,129},{4... | collective-permute-start | bytes 98312 | tf_op jit(solution)/shard_map/ppermute | solution.py:29
  140.5 1.2 collective-permute-start.16
  164.6 1.5 collective-permute-start.17
  (9 other events, 35.9 us)

commit v5 on v4

--- a/solution.py
+++ b/solution.py
@@ -284,7 +284,8 @@
     partial = teacher(far, *chip)
     partial = teacher(far, *next_chip, partial, kept=jnp.bfloat16)
     there = swap(partial, FAR)
-    opposite = swap(near_half(spot, far), NEAR)
+    later_far, partial = tie(far, partial)
+    opposite = swap(near_half(spot, later_far), NEAR)
     later_own, _ = tie(own, partial)
     here = teacher(later_own, *next_chip, here)
     there, here, near = tie(there, here, near)

time: 170 us -> 169 us (level)
  no operation moved by 1% of the time
where the time goes in v5:
time: 169 us; the launch traced here: 166 us
  waiting for transfers between devices  64.2 us (38%)
  starting transfers between devices  43.7 us (26%)
  Pallas kernels  25.1 us (15%)
  blocking collectives  16.7 us (10%)
  other arithmetic  7.8 us (5%)
  local copies, waits for them, and re-layouts  5.12 us (3%)
  matrix products  2.87 us (2%)
    ppermute x18, waiting for transfers between devices, swap(): lax.ppermute(values, LINE, [(index, index ^ mask) for index in range(8)])  28.8 us
    all_to_all x1, waiting for transfers between devices, shards(): lax.all_to_all(ordered.reshape(tables, samples, width), 'dp', split_axis=...  25.3 us
    all_to_all x1, blocking collectives, across(): return lax.all_to_all(values, 'dp', split_axis=0, concat_axis=0, tiled=True)  16.7 us
    ppermute x18, starting transfers between devices, swap(): lax.ppermute(values, LINE, [(index, index ^ mask) for index in range(8)])  16.4 us
    all_to_all x2, starting transfers between devices, across(): return lax.all_to_all(values, 'dp', split_axis=0, concat_axis=0, tiled=True)  16 us
    pallas_call x4, Pallas kernels, teacher(): pl.pallas_call(teacher_kernel, out_shape=jax.ShapeDtypeStruct((features.s...  12.4 us
    all_to_all x1, starting transfers between devices, shards(): lax.all_to_all(ordered.reshape(tables, samples, width), 'dp', split_axis=...  11.4 us
    all_to_all x2, waiting for transfers between devices, across(): return lax.all_to_all(values, 'dp', split_axis=0, concat_axis=0, tiled=True)  10.1 us
  transfers between devices with their start and end apart: 21, of which 13 were waited for; matrix products, arithmetic and copies ran while one was open for 6% of the time, Pallas kernels for 15%

profile of v5, /device:TPU:32, one launch (start us, length us, event | category | flops | bytes accessed | tf_op | source)
XLA Modules:
  0.0 166.4 jit_solution(13014574047832389507)
XLA Ops:
  3.0 1.8 %convert_divide_fusion.averaged_ref = f32[4096,128]{1,0:T(8,128)S(1)} fusion(bf16[1,1,4096,128]{3,2,1,0:T(8,128)(2,1)} %param.9, f32[4096]{0:T(1024)S(1)} %bitcast.26), kind=kLoop, calls=%fused_computation | loop fusion | flops 1048576 | bytes 3162112 | tf_op jit(solution)/shard_map/div | solution.py:258
  4.8 5.5 %take_rows.1 = bf16[4096,128]{1,0:T(8,128)(2,1)} custom-call(s32[1,4096]{1,0:T(1,128)S(1)} %copy-done.9, f32[4096,128]{1,0:T(8,128)S(1)} %convert_divide_fusion.averaged_ref), custom_call_target="tpu_custom_call" | custom-call | tf_op jit(solution)/shard_map/take_rows/pallas_call | solution.py:57
  10.2 11.4 %all-to-all-start = ((bf16[32,128,128]{2,1,0:T(8,128)(2,1)}), bf16[32,128,128]{2,1,0:T(8,128)(2,1)S(1)}, u32[]{:S(2)}, u32[]{:S(2)}) async-start(bf16[32,128,128]{2,1,0:T(8,128)(2,1)} %bitcast.5), calls=%async_computation | async-start | bytes 2097152 | tf_op jit(solution)/shard_map/all_to_all | solution.py:260
  21.7 1.9 %fusion = (bf16[256,512]{1,0:T(8,128)(2,1)S(1)}, f32[256,512]{1,0:T(8,128)S(1)}) fusion(bf16[256,2048]{1,0:T(8,128)(2,1)} %param.14, bf16[2048,512]{1,0:T(8,128)(2,1)S(1)} %copy-done), kind=kOutput, calls=%fused_computation.14 | convolution fusion | flops 537001984 | bytes 3932160 | tf_op jit(solution)/shard_map/dot_general | solution.py:25
  24.6 25.3 %all-to-all-done.arrived_ref = bf16[32,128,128]{2,1,0:T(8,128)(2,1)S(1)} async-done(((bf16[32,128,128]{2,1,0:T(8,128)(2,1)}), bf16[32,128,128]{2,1,0:T(8,128)(2,1)S(1)}, u32[]{:S(2)}, u32[]{:S(2)}) %all-to-all-start) | async-done | bytes 1048608 | tf_op jit(solution)/shard_map/all_to_all | solution.py:260
  51.5 2.2 %collective-permute-start.1 = (bf16[128,4096]{1,0:T(8,128)(2,1)S(1)}, bf16[128,4096]{1,0:T(8,128)(2,1)S(1)}, u32[]{:S(2)}, u32[]{:S(2)}) collective-permute-start(bf16[128,4096]{1,0:T(8,128)(2,1)S(1)} %get-tuple-element.30.features_ref.refs_0_), channel_id=1, source_target_pairs={{0,130},{1,131},{2,128},{3,129},{128,2},{129,3},{130,0},{131,1},{4... | collective-permute-start | bytes 3145736 | tf_op jit(solution)/shard_map/ppermute | solution.py:29
  56.7 3.0 %teacher.4.refs_4_ = f32[128,512]{1,0:T(8,128)S(1)} custom-call(bf16[128,4096]{1,0:T(8,128)(2,1)S(1)} %get-tuple-element.30.features_ref.refs_0_, bf16[512,512]{1,0:T(8,128)(2,1)} %pad_maximum_fusion.refs_0_, bf16[512,512]{1,0:T(8,128)(2,1)} %collective-permute-done.3.refs_1_, bf16[4096,256]{1,0:T(8,128)(2,1)S(1)} %copy-done.3, ...), custom_call_target="tpu_custom_call" | custom-call | tf_op jit(solution)/shard_map/teacher/pallas_call | solution.py:123
  61.1 6.4 %collective-permute-done.2.refs_0_ = bf16[512,512]{1,0:T(8,128)(2,1)S(1)} collective-permute-done((bf16[512,512]{1,0:T(8,128)(2,1)}, bf16[512,512]{1,0:T(8,128)(2,1)S(1)}, u32[]{:S(2)}, u32[]{:S(2)}) %collective-permute-start.2) | collective-permute-done | bytes 524320 | tf_op jit(solution)/shard_map/ppermute | solution.py:29
  67.5 10.4 %collective-permute-done.1.features_ref.refs_2_ = bf16[128,4096]{1,0:T(8,128)(2,1)S(1)} collective-permute-done((bf16[128,4096]{1,0:T(8,128)(2,1)S(1)}, bf16[128,4096]{1,0:T(8,128)(2,1)S(1)}, u32[]{:S(2)}, u32[]{:S(2)}) %collective-permute-start.1) | collective-permute-done | bytes 1048608 | tf_op jit(solution)/shard_map/ppermute | solution.py:29
  77.9 3.0 %teacher.5.refs_4_ = f32[128,512]{1,0:T(8,128)S(1)} custom-call(bf16[128,4096]{1,0:T(8,128)(2,1)S(1)} %collective-permute-done.1.features_ref.refs_2_, bf16[512,512]{1,0:T(8,128)(2,1)} %pad_maximum_fusion.refs_0_, bf16[512,512]{1,0:T(8,128)(2,1)} %collective-permute-done.3.refs_1_, bf16[4096,256]{1,0:T(8,128)(2,1)S(1)} %copy-done.4, ...), custom_call_target="tpu_custom_call" | custom-call | tf_op jit(solution)/shard_map/teacher/pallas_call | solution.py:123
  80.9 3.2 %teacher.6 = bf16[128,512]{1,0:T(8,128)(2,1)S(1)} custom-call(bf16[128,4096]{1,0:T(8,128)(2,1)S(1)} %collective-permute-done.1.features_ref.refs_2_, bf16[512,512]{1,0:T(8,128)(2,1)S(1)} %collective-permute-done.2.refs_0_, bf16[512,512]{1,0:T(8,128)(2,1)S(1)} %collective-permute-done.5.refs_1_, bf16[4096,256]{1,0:T(8,128)(2,1)} %collective-permute-done.refs_2_, ...), custom_call_target="tpu_custom_call" | custom-call | tf_op jit(solution)/shard_map/teacher/pallas_call | solution.py:123
  85.6 2.0 %collective-permute-start.7 = (bf16[128,2048]{1,0:T(8,128)(2,1)}, bf16[128,2048]{1,0:T(8,128)(2,1)}, u32[]{:S(2)}, u32[]{:S(2)}) collective-permute-start(bf16[128,2048]{1,0:T(8,128)(2,1)} %near_half.1), channel_id=1, source_target_pairs={{0,128},{1,129},{2,130},{3,131},{128,0},{129,1},{130,2},{131,3},{4... | collective-permute-start | bytes 1572872 | tf_op jit(solution)/shard_map/ppermute | solution.py:29
  87.6 2.1 %collective-permute-start.8 = (bf16[128,512]{1,0:T(8,128)(2,1)S(1)}, bf16[128,512]{1,0:T(8,128)(2,1)S(1)}, u32[]{:S(2)}, u32[]{:S(2)}) collective-permute-start(bf16[128,512]{1,0:T(8,128)(2,1)S(1)} %teacher.6), channel_id=1, source_target_pairs={{0,130},{1,131},{2,128},{3,129},{128,2},{129,3},{130,0},{131,1},{4... | collective-permute-start | bytes 393224 | tf_op jit(solution)/shard_map/ppermute | solution.py:29
  89.7 3.2 %teacher.7.refs_1_ = f32[128,512]{1,0:T(8,128)S(1)} custom-call(bf16[128,4096]{1,0:T(8,128)(2,1)S(1)} %get-tuple-element.30.features_ref.refs_0_, bf16[512,512]{1,0:T(8,128)(2,1)S(1)} %collective-permute-done.2.refs_0_, bf16[512,512]{1,0:T(8,128)(2,1)S(1)} %collective-permute-done.5.refs_1_, bf16[4096,256]{1,0:T(8,128)(2,1)} %collective-permute-done.refs_2_, ...), custom_call_target="tpu_custom_call" | custom-call | tf_op jit(solution)/shard_map/teacher/pallas_call | solution.py:123
  95.9 10.2 %all-to-all-start.1 = ((bf16[32,16,512]{2,1,0:T(8,128)(2,1)}), bf16[32,16,512]{2,1,0:T(8,128)(2,1)}, u32[]{:S(2)}, u32[]{:S(2)}) async-start(bf16[32,16,512]{2,1,0:T(8,128)(2,1)} %bitcast.25), calls=%async_computation.1 | async-start | bytes 1048576 | tf_op jit(solution)/shard_map/all_to_all | solution.py:39
  107.4 1.6 collective-permute-start.11
  116.2 1.9 %collective-permute-done.13 = bf16[512,512]{1,0:T(8,128)(2,1)S(1)} collective-permute-done((bf16[512,512]{1,0:T(8,128)(2,1)S(1)}, bf16[512,512]{1,0:T(8,128)(2,1)S(1)}, u32[]{:S(2)}, u32[]{:S(2)}) %collective-permute-start.13) | collective-permute-done | bytes 524320 | tf_op jit(solution)/shard_map/ppermute | solution.py:29
  119.1 4.0 %all-to-all-done.1 = bf16[32,16,512]{2,1,0:T(8,128)(2,1)} async-done(((bf16[32,16,512]{2,1,0:T(8,128)(2,1)}), bf16[32,16,512]{2,1,0:T(8,128)(2,1)}, u32[]{:S(2)}, u32[]{:S(2)}) %all-to-all-start.1) | async-done | bytes 524320 | tf_op jit(solution)/shard_map/all_to_all | solution.py:39
  123.0 5.8 %all-to-all-start.2 = ((bf16[32,16,512]{2,1,0:T(8,128)(2,1)}), bf16[32,16,512]{2,1,0:T(8,128)(2,1)S(1)}, u32[]{:S(2)}, u32[]{:S(2)}) async-start(bf16[32,16,512]{2,1,0:T(8,128)(2,1)} %bitcast.9), calls=%async_computation.2 | async-start | bytes 1048576 | tf_op jit(solution)/shard_map/all_to_all | solution.py:39
  131.3 2.7 %collective-permute-done.14 = f32[16,512]{1,0:T(8,128)S(1)} collective-permute-done((f32[16,512]{1,0:T(8,128)S(1)}, f32[16,512]{1,0:T(8,128)S(1)}, u32[]{:S(2)}, u32[]{:S(2)}) %collective-permute-start.14) | collective-permute-done | bytes 32800 | tf_op jit(solution)/shard_map/ppermute | solution.py:29
  134.0 2.3 %collective-permute-start.15 = (f32[16,512]{1,0:T(8,128)S(1)}, f32[16,512]{1,0:T(8,128)S(1)}, u32[]{:S(2)}, u32[]{:S(2)}) collective-permute-start(f32[16,512]{1,0:T(8,128)S(1)} %add.22), channel_id=1, source_target_pairs={{0,2},{1,3},{2,0},{3,1},{128,130},{129,131},{130,128},{131,129},{4... | collective-permute-start | bytes 98312 | tf_op jit(solution)/shard_map/ppermute | solution.py:29
  136.3 3.2 %collective-permute-done.15 = f32[16,512]{1,0:T(8,128)S(1)} collective-permute-done((f32[16,512]{1,0:T(8,128)S(1)}, f32[16,512]{1,0:T(8,128)S(1)}, u32[]{:S(2)}, u32[]{:S(2)}) %collective-permute-start.15) | collective-permute-done | bytes 32800 | tf_op jit(solution)/shard_map/ppermute | solution.py:29
  140.6 6.2 %all-to-all-done.2 = bf16[32,16,512]{2,1,0:T(8,128)(2,1)S(1)} async-done(((bf16[32,16,512]{2,1,0:T(8,128)(2,1)}), bf16[32,16,512]{2,1,0:T(8,128)(2,1)S(1)}, u32[]{:S(2)}, u32[]{:S(2)}) %all-to-all-start.2) | async-done | bytes 524320 | tf_op jit(solution)/shard_map/all_to_all | solution.py:39
  146.8 16.7 %all_to_all.34 = bf16[32,8,512]{2,1,0:T(8,128)(2,1)S(1)} all-to-all(bf16[32,8,512]{2,1,0:T(8,128)(2,1)S(1)} %broadcast_in_dim.24), channel_id=1, replica_groups=mesh['grp'=2,'dp'=32,'mp'=4] {'dp'}, dimensions={0} | all-to-all | bytes 524288 | tf_op jit(solution)/shard_map/all_to_all | solution.py:39
  (73 shorter events, 29.8 us)
Async XLA Ops:
  0.6 21.1 %copy-start = (bf16[2048,512]{1,0:T(8,128)(2,1)S(1)}, bf16[2048,512]{1,0:T(8,128)(2,1)}, u32[]{:S(2)}) copy-start(bf16[2048,512]{1,0:T(8,128)(2,1)} %param.15) | copy-start | bytes 6291460
  0.7 49.2 %collective-permute-start = (bf16[4096,256]{1,0:T(8,128)(2,1)}, bf16[4096,256]{1,0:T(8,128)(2,1)}, u32[]{:S(2)}, u32[]{:S(2)}) collective-permute-start(bf16[4096,256]{1,0:T(8,128)(2,1)} %refs_2_.3), channel_id=1, source_target_pairs={{0,128},{1,129},{2,130},{3,131},{128,0},{129,1},{130,2},{131,3},{4... | collective-permute-start | bytes 6291464 | tf_op jit(solution)/shard_map/ppermute | solution.py:29
  10.2 39.6 %all-to-all-start = ((bf16[32,128,128]{2,1,0:T(8,128)(2,1)}), bf16[32,128,128]{2,1,0:T(8,128)(2,1)S(1)}, u32[]{:S(2)}, u32[]{:S(2)}) async-start(bf16[32,128,128]{2,1,0:T(8,128)(2,1)} %bitcast.5), calls=%async_computation | async-start | bytes 2097152 | tf_op jit(solution)/shard_map/all_to_all | solution.py:260
  21.6 28.8 %copy-start.11 = (s32[32]{0:T(128)S(1)}, s32[32]{0:T(128)}, u32[]{:S(2)}) copy-start(s32[32]{0:T(128)} %param.12) | copy-start | bytes 388
  21.6 33.5 %collective-permute-start.4 = (bf16[4096,256]{1,0:T(8,128)(2,1)}, bf16[4096,256]{1,0:T(8,128)(2,1)}, u32[]{:S(2)}, u32[]{:S(2)}) collective-permute-start(bf16[4096,256]{1,0:T(8,128)(2,1)} %refs_2_.3), channel_id=1, source_target_pairs={{0,1},{1,0},{2,3},{3,2},{128,129},{129,128},{130,131},{131,130},{4... | collective-permute-start | bytes 6291464 | tf_op jit(solution)/shard_map/ppermute | solution.py:29
  49.8 31.0 %collective-permute-start.6 = (bf16[4096,256]{1,0:T(8,128)(2,1)}, bf16[4096,256]{1,0:T(8,128)(2,1)}, u32[]{:S(2)}, u32[]{:S(2)}) collective-permute-start(bf16[4096,256]{1,0:T(8,128)(2,1)} %collective-permute-done.refs_2_), channel_id=1, source_target_pairs={{0,1},{1,0},{2,3},{3,2},{128,129},{129,128},{130,131},{131,130},{4... | collective-permute-start | bytes 6291464 | tf_op jit(solution)/shard_map/ppermute | solution.py:29
  49.9 5.2 %collective-permute-start.3 = (bf16[512,512]{1,0:T(8,128)(2,1)}, bf16[512,512]{1,0:T(8,128)(2,1)}, u32[]{:S(2)}, u32[]{:S(2)}) collective-permute-start(bf16[512,512]{1,0:T(8,128)(2,1)} %pad_maximum_fusion.refs_0_), channel_id=1, source_target_pairs={{0,1},{1,0},{2,3},{3,2},{128,129},{129,128},{130,131},{131,130},{4... | collective-permute-start | bytes 1572872 | tf_op jit(solution)/shard_map/ppermute | solution.py:29
  51.5 38.2 %copy-start.1 = (bf16[128,4096]{1,0:T(8,128)(2,1)}, bf16[128,4096]{1,0:T(8,128)(2,1)S(1)}, u32[]{:S(2)}) copy-start(bf16[128,4096]{1,0:T(8,128)(2,1)S(1)} %get-tuple-element.30.features_ref.refs_0_) | copy-start | bytes 3145732
  51.5 26.4 %collective-permute-start.1 = (bf16[128,4096]{1,0:T(8,128)(2,1)S(1)}, bf16[128,4096]{1,0:T(8,128)(2,1)S(1)}, u32[]{:S(2)}, u32[]{:S(2)}) collective-permute-start(bf16[128,4096]{1,0:T(8,128)(2,1)S(1)} %get-tuple-element.30.features_ref.refs_0_), channel_id=1, source_target_pairs={{0,130},{1,131},{2,128},{3,129},{128,2},{129,3},{130,0},{131,1},{4... | collective-permute-start | bytes 3145736 | tf_op jit(solution)/shard_map/ppermute | solution.py:29
  53.7 13.8 %collective-permute-start.2 = (bf16[512,512]{1,0:T(8,128)(2,1)}, bf16[512,512]{1,0:T(8,128)(2,1)S(1)}, u32[]{:S(2)}, u32[]{:S(2)}) collective-permute-start(bf16[512,512]{1,0:T(8,128)(2,1)} %pad_maximum_fusion.refs_0_), channel_id=1, source_target_pairs={{0,128},{1,129},{2,130},{3,131},{128,0},{129,1},{130,2},{131,3},{4... | collective-permute-start | bytes 1572872 | tf_op jit(solution)/shard_map/ppermute | solution.py:29
  77.9 3.0 %collective-permute-start.5 = (bf16[512,512]{1,0:T(8,128)(2,1)S(1)}, bf16[512,512]{1,0:T(8,128)(2,1)S(1)}, u32[]{:S(2)}, u32[]{:S(2)}) collective-permute-start(bf16[512,512]{1,0:T(8,128)(2,1)S(1)} %collective-permute-done.2.refs_0_), channel_id=1, source_target_pairs={{0,1},{1,0},{2,3},{3,2},{128,129},{129,128},{130,131},{131,130},{4... | collective-permute-start | bytes 1572872 | tf_op jit(solution)/shard_map/ppermute | solution.py:29
  77.9 15.1 %collective-permute-start.9 = (bf16[128,2048]{1,0:T(8,128)(2,1)S(1)}, bf16[128,2048]{1,0:T(8,128)(2,1)S(1)}, u32[]{:S(2)}, u32[]{:S(2)}) collective-permute-start(bf16[128,2048]{1,0:T(8,128)(2,1)S(1)} %get-tuple-element.37), channel_id=1, source_target_pairs={{0,128},{1,129},{2,130},{3,131},{128,0},{129,1},{130,2},{131,3},{4... | collective-permute-start | bytes 1572872 | tf_op jit(solution)/shard_map/ppermute | solution.py:29
  85.6 27.6 %collective-permute-start.7 = (bf16[128,2048]{1,0:T(8,128)(2,1)}, bf16[128,2048]{1,0:T(8,128)(2,1)}, u32[]{:S(2)}, u32[]{:S(2)}) collective-permute-start(bf16[128,2048]{1,0:T(8,128)(2,1)} %near_half.1), channel_id=1, source_target_pairs={{0,128},{1,129},{2,130},{3,131},{128,0},{129,1},{130,2},{131,3},{4... | collective-permute-start | bytes 1572872 | tf_op jit(solution)/shard_map/ppermute | solution.py:29
  87.6 6.6 %collective-permute-start.8 = (bf16[128,512]{1,0:T(8,128)(2,1)S(1)}, bf16[128,512]{1,0:T(8,128)(2,1)S(1)}, u32[]{:S(2)}, u32[]{:S(2)}) collective-permute-start(bf16[128,512]{1,0:T(8,128)(2,1)S(1)} %teacher.6), channel_id=1, source_target_pairs={{0,130},{1,131},{2,128},{3,129},{128,2},{129,3},{130,0},{131,1},{4... | collective-permute-start | bytes 393224 | tf_op jit(solution)/shard_map/ppermute | solution.py:29
  95.9 27.1 %all-to-all-start.1 = ((bf16[32,16,512]{2,1,0:T(8,128)(2,1)}), bf16[32,16,512]{2,1,0:T(8,128)(2,1)}, u32[]{:S(2)}, u32[]{:S(2)}) async-start(bf16[32,16,512]{2,1,0:T(8,128)(2,1)} %bitcast.25), calls=%async_computation.1 | async-start | bytes 1048576 | tf_op jit(solution)/shard_map/all_to_all | solution.py:39
  106.1 8.4 %collective-permute-start.12 = (bf16[128,512]{1,0:T(8,128)(2,1)S(1)}, bf16[128,512]{1,0:T(8,128)(2,1)S(1)}, u32[]{:S(2)}, u32[]{:S(2)}) collective-permute-start(bf16[128,512]{1,0:T(8,128)(2,1)S(1)} %get-tuple-element.44.refs_0_), channel_id=1, source_target_pairs={{0,2},{1,3},{2,0},{3,1},{128,130},{129,131},{130,128},{131,129},{4... | collective-permute-start | bytes 393224 | tf_op jit(solution)/shard_map/ppermute | solution.py:29
  107.4 7.1 %collective-permute-start.11 = (bf16[128,512]{1,0:T(8,128)(2,1)S(1)}, bf16[128,512]{1,0:T(8,128)(2,1)S(1)}, u32[]{:S(2)}, u32[]{:S(2)}) collective-permute-start(bf16[128,512]{1,0:T(8,128)(2,1)S(1)} %get-tuple-element.44.refs_0_), channel_id=1, source_target_pairs={{0,130},{1,131},{2,128},{3,129},{128,2},{129,3},{130,0},{131,1},{4... | collective-permute-start | bytes 393224 | tf_op jit(solution)/shard_map/ppermute | solution.py:29
  109.0 5.5 %collective-permute-start.10 = (bf16[128,512]{1,0:T(8,128)(2,1)S(1)}, bf16[128,512]{1,0:T(8,128)(2,1)S(1)}, u32[]{:S(2)}, u32[]{:S(2)}) collective-permute-start(bf16[128,512]{1,0:T(8,128)(2,1)S(1)} %get-tuple-element.44.refs_0_), channel_id=1, source_target_pairs={{0,128},{1,129},{2,130},{3,131},{128,0},{129,1},{130,2},{131,3},{4... | collective-permute-start | bytes 393224 | tf_op jit(solution)/shard_map/ppermute | solution.py:29
  116.1 2.0 %collective-permute-start.13 = (bf16[512,512]{1,0:T(8,128)(2,1)S(1)}, bf16[512,512]{1,0:T(8,128)(2,1)S(1)}, u32[]{:S(2)}, u32[]{:S(2)}) collective-permute-start(bf16[512,512]{1,0:T(8,128)(2,1)S(1)} %get-tuple-element.46), channel_id=1, source_target_pairs={{0,1},{1,0},{2,3},{3,2},{128,129},{129,128},{130,131},{131,130},{4... | collective-permute-start | bytes 1572872 | tf_op jit(solution)/shard_map/ppermute | solution.py:29
  123.0 23.8 %all-to-all-start.2 = ((bf16[32,16,512]{2,1,0:T(8,128)(2,1)}), bf16[32,16,512]{2,1,0:T(8,128)(2,1)S(1)}, u32[]{:S(2)}, u32[]{:S(2)}) async-start(bf16[32,16,512]{2,1,0:T(8,128)(2,1)} %bitcast.9), calls=%async_computation.2 | async-start | bytes 1048576 | tf_op jit(solution)/shard_map/all_to_all | solution.py:39
  130.0 4.0 %collective-permute-start.14 = (f32[16,512]{1,0:T(8,128)S(1)}, f32[16,512]{1,0:T(8,128)S(1)}, u32[]{:S(2)}, u32[]{:S(2)}) collective-permute-start(f32[16,512]{1,0:T(8,128)S(1)} %convert_reduce_fusion.1), channel_id=1, source_target_pairs={{0,128},{1,129},{2,130},{3,131},{128,0},{129,1},{130,2},{131,3},{4... | collective-permute-start | bytes 98312 | tf_op jit(solution)/shard_map/ppermute | solution.py:29
  134.0 5.4 %collective-permute-start.15 = (f32[16,512]{1,0:T(8,128)S(1)}, f32[16,512]{1,0:T(8,128)S(1)}, u32[]{:S(2)}, u32[]{:S(2)}) collective-permute-start(f32[16,512]{1,0:T(8,128)S(1)} %add.22), channel_id=1, source_target_pairs={{0,2},{1,3},{2,0},{3,1},{128,130},{129,131},{130,128},{131,129},{4... | collective-permute-start | bytes 98312 | tf_op jit(solution)/shard_map/ppermute | solution.py:29
  139.4 1.2 collective-permute-start.16
  163.5 1.5 collective-permute-start.17
  (9 other events, 33.2 us)
